TPU v7x, 256 devices: a whole 4x4x8 slice. The times are simulated.
256 devices in a mesh: tm: 32 (over y, z_hi, x), dp: 8 (over z_lo, core).
Axes of the slice: x: 4, y: 4, z: 8 (z_hi: 2, z_lo: 4; z = z_hi * 4 + z_lo), core: 2. Of those that a mesh axis runs over, the one named last changes fastest.
Arguments:
- queries: bfloat16 [8, 8192, 1664], P('dp', 'tm'), may hold values from -5 to 5
- keys: bfloat16 [8, 8192, 1664], P('dp', 'tm'), may hold values from -5 to 5
- values: bfloat16 [8, 8192, 1664], P('dp', 'tm'), may hold values from -6 to 6
- grad_out: bfloat16 [8, 8192, 3200], P('dp', 'tm'), may hold values from -1.5 to 1.5
- out_weight: bfloat16 [1664, 3200], P(None, 'dp'), may hold values from -0.15625 to 0.15625
- frame_clip: int32 [8, 32], P('dp'), may hold values from 0 to 4, never falling along the last dimension, each value on 1 to 12 neighbouring positions
Outputs:
- result: bfloat16 [8, 8192, 3200], P('dp', 'tm')
- grad_queries: bfloat16 [8, 8192, 1664], P('dp', 'tm')
- grad_keys: bfloat16 [8, 8192, 1664], P('dp', 'tm')
- grad_values: bfloat16 [8, 8192, 1664], P('dp', 'tm')
- grad_weight: bfloat16 [1664, 3200], P('tm', 'dp')
All inputs are finite; a program needn't handle non-finite values.
Results may differ from a plain program's by a relative error of at most 0.025.
Values may be sent and summed in bfloat16 or wider, within the bound.
A program may use at most 192 MiB of HBM per device.

v0:
```python
import jax
import jax.numpy as jnp
from jax import lax
from jax.sharding import PartitionSpec as P

HS = 128
P_SIZE = 256


def padded_2(block, sides, width):
    for axis, dim in sides:
        count = lax.axis_size(axis)
        forward = [(i, i + 1) for i in range(count - 1)]
        backward = [(target, source) for source, target in forward]
        low = lax.ppermute(
            lax.slice_in_dim(block, block.shape[dim] - width, None, axis=dim), axis, forward
        )
        high = lax.ppermute(lax.slice_in_dim(block, 0, width, axis=dim), axis, backward)
        block = jnp.concatenate([low, block, high], axis=dim)
    return block


def passed_along(block, axis, distance):
    devices = range(lax.axis_size(axis))
    route = [(i - distance, i) for i in devices if i - distance in devices]
    return lax.ppermute(block, axis, route)


def frame_scores(query_frame, key_window, allowed):
    scores = jnp.einsum(
        "qhd,khd->hqk", query_frame, key_window, preferred_element_type=jnp.float32
    ) * HS ** (-0.5)
    live = jnp.repeat(allowed, P_SIZE)[None, None, :]
    return (scores, live)


def attend(query_frame, key_window, value_window, allowed):
    scores, live = frame_scores(query_frame, key_window, allowed)
    peak = jnp.max(jnp.where(live, scores, -1e30), axis=-1, keepdims=True)
    expo = jnp.where(live, jnp.exp(scores - peak), 0.0)
    total = jnp.sum(expo, axis=-1, keepdims=True)
    weights = (expo / total).astype(jnp.bfloat16)
    mixed = jnp.einsum(
        "hqk,khd->qhd", weights, value_window, preferred_element_type=jnp.float32
    ).astype(jnp.bfloat16)
    return (mixed, (peak + jnp.log(total))[..., 0])


def backprop(query_frame, key_window, value_window, allowed, grad_frame, lse, delta):
    scores, live = frame_scores(query_frame, key_window, allowed)
    probs = jnp.where(live, jnp.exp(scores - lse[..., None]), 0.0)
    grad_vals = jnp.einsum(
        "hqk,qhd->khd", probs.astype(jnp.bfloat16), grad_frame, preferred_element_type=jnp.float32
    )
    grad_probs = jnp.einsum(
        "qhd,khd->hqk", grad_frame, value_window, preferred_element_type=jnp.float32
    )
    rounded = (probs * (grad_probs - delta[..., None])).astype(jnp.bfloat16)
    grad_query = jnp.einsum(
        "hqk,khd->qhd", rounded, key_window, preferred_element_type=jnp.float32
    ) * HS ** (-0.5)
    grad_key = jnp.einsum(
        "hqk,qhd->khd", rounded, query_frame, preferred_element_type=jnp.float32
    ) * HS ** (-0.5)
    return (grad_query, grad_key, grad_vals)


def windows(padded):
    return jnp.concatenate([padded[:-2], padded[1:-1], padded[2:]], axis=1)


def spread_back(window):
    parts = [window[:, t * P_SIZE : (t + 1) * P_SIZE] for t in range(3)]
    total = jnp.pad(parts[0], ((0, 2), (0, 0), (0, 0), (0, 0)))
    total = total + jnp.pad(parts[1], ((1, 1), (0, 0), (0, 0), (0, 0)))
    return total + jnp.pad(parts[2], ((2, 0), (0, 0), (0, 0), (0, 0)))


def on_device(queries, keys, values, grad_out, out_weight, frame_clip):
    rows = queries.shape[1]
    width = queries.shape[2]
    heads = width // HS
    frames = rows // P_SIZE
    place = lax.axis_index("tm") * frames
    clip_all = frame_clip[0]
    extended = jnp.pad(clip_all, 1, constant_values=-1)
    own_clip = lax.dynamic_slice_in_dim(clip_all, place, frames)
    near_clip = lax.dynamic_slice_in_dim(extended, place, frames + 2)
    allowed = (
        jnp.stack([near_clip[:-2], near_clip[1:-1], near_clip[2:]], axis=1) == own_clip[:, None]
    )
    paired = jnp.stack([keys[0], values[0]])
    padded = padded_2(paired, (("tm", 1),), P_SIZE)
    key_pad = padded[0].reshape(frames + 2, P_SIZE, heads, HS)
    value_pad = padded[1].reshape(frames + 2, P_SIZE, heads, HS)
    key_win = windows(key_pad)
    value_win = windows(value_pad)
    query_frames = queries[0].reshape(frames, P_SIZE, heads, HS)
    mixed, lse = lax.map(lambda t: attend(*t), (query_frames, key_win, value_win, allowed))
    mixed_rows = mixed.reshape(rows, width)
    full_weight = lax.all_gather(out_weight, "dp", axis=1, tiled=True)
    result = jnp.dot(mixed_rows, full_weight, preferred_element_type=jnp.float32).astype(
        jnp.bfloat16
    )
    grad_rows = grad_out[0]
    grad_mixed = lax.dot_general(
        grad_rows, full_weight, (((1,), (1,)), ((), ())), preferred_element_type=jnp.float32
    ).astype(jnp.bfloat16)
    share = lax.psum_scatter(
        lax.dot_general(
            mixed_rows, grad_rows, (((0,), (0,)), ((), ())), preferred_element_type=jnp.float32
        ).astype(jnp.bfloat16),
        "tm",
        scatter_dimension=0,
        tiled=True,
    ).astype(jnp.float32)
    weight_grad = lax.psum_scatter(share, "dp", scatter_dimension=1, tiled=True)
    grad_frames = grad_mixed.reshape(frames, P_SIZE, heads, HS)
    delta = jnp.einsum("fqhd,fqhd->fhq", grad_frames, mixed, preferred_element_type=jnp.float32)
    grad_q, grad_kw, grad_vw = lax.map(
        lambda t: backprop(*t), (query_frames, key_win, value_win, allowed, grad_frames, lse, delta)
    )
    key_spread = spread_back(grad_kw)
    value_spread = spread_back(grad_vw)
    own = jnp.stack([key_spread[1:-1], value_spread[1:-1]])
    lower = jnp.stack([key_spread[0], value_spread[0]])
    upper = jnp.stack([key_spread[-1], value_spread[-1]])
    from_above = passed_along(lower, "tm", -1)
    from_below = passed_along(upper, "tm", 1)
    own = own.at[:, 0].add(from_below).at[:, -1].add(from_above)
    grad_queries = grad_q.reshape(1, rows, width).astype(jnp.bfloat16)
    grad_keys = own[0].reshape(1, rows, width).astype(jnp.bfloat16)
    grad_values = own[1].reshape(1, rows, width).astype(jnp.bfloat16)
    return (result[None], grad_queries, grad_keys, grad_values, weight_grad.astype(jnp.bfloat16))


def solution(mesh):
    in_specs = (
        P("dp", "tm", None),
        P("dp", "tm", None),
        P("dp", "tm", None),
        P("dp", "tm", None),
        P(None, "dp"),
        P("dp", None),
    )
    out_specs = (
        P("dp", "tm", None),
        P("dp", "tm", None),
        P("dp", "tm", None),
        P("dp", "tm", None),
        P("tm", "dp"),
    )
    return jax.shard_map(
        on_device, mesh=mesh, in_specs=in_specs, out_specs=out_specs, check_vma=False
    )
```

profile of v0, /device:TPU:37, one launch (start us, length us, event | category | flops | bytes accessed | tf_op | source)
XLA Modules:
  0.0 893.0 jit_solution(9635594737787634751)
XLA Ops:
  8.0 1.5 copy.49
  9.5 1.5 copy.50
  11.1 1.5 pad_maximum_fusion.2
  12.5 2.2 collective-permute-start.1
  14.7 3.1 collective-permute-start
  19.2 1.3 copy.54
  20.6 2.2 copy.56
  22.8 30.0 %collective-permute-done.1 = bf16[2,256,1664]{1,2,0:T(8,128)(2,1)} collective-permute-done((bf16[2,256,1664]{1,2,0:T(8,128)(2,1)}, bf16[2,256,1664]{1,2,0:T(8,128)(2,1)}, u32[]{:S(2)}, u32[]{:S(2)}) %collective-permute-start.1) | collective-permute-done | bytes 1703968 | tf_op jit(solution)/shard_map/ppermute | solution.py:18
  52.8 2.4 fusion.35
  56.6 2.4 fusion.34
  60.3 4.7 select_reduce_fusion
  65.0 2.1 bitcast_reduce_fusion
  67.1 1.7 copy-done.1
  68.8 57.2 %all-gather.2.cloned.1.call-done = bf16[1664,3200]{0,1:T(8,128)(2,1)} async-done(((bf16[1664,400]{0,1:T(8,128)(2,1)}), bf16[1664,3200]{0,1:T(8,128)(2,1)}) %all-gather.2.cloned.1.call-update) | async-done | bytes 10649616 | tf_op jit(solution)/shard_map/all_gather | solution.py:101
  126.0 8.2 convolution_convert_fusion.2
  134.2 1.5 copy.59
  135.8 5.6 fusion.13
  141.4 1.5 copy-done.2
  143.3 3.8 fusion.14
  147.1 6.2 fusion.1
  153.3 3.7 multiply_bitcast_fusion
  159.4 3.0 fusion.29
  162.3 4.3 pad_maximum_fusion
  166.6 76.0 %collective-permute-start.2 = (f32[2,256,13,128]{1,3,2,0:T(8,128)}, f32[2,256,13,128]{1,3,2,0:T(8,128)}, u32[]{:S(2)}, u32[]{:S(2)}) collective-permute-start(f32[2,256,13,128]{1,3,2,0:T(8,128)} %pad_maximum_fusion), channel_id=1, source_target_pairs={{0,8},{8,16},{16,24},{24,32},{32,40},{40,48},{48,56},{56,64},{64,7... | collective-permute-start | bytes 10223624 | tf_op jit(solution)/shard_map/ppermute | solution.py:26
  242.6 1.9 pad_maximum_fusion.1
  244.5 1.9 collective-permute-start.3
  246.4 5.6 convolution_convert_fusion
  252.0 387.3 %fusion = bf16[64,3200]{1,0:T(8,128)(2,1)} fusion(bf16[1664,3200]{1,0:T(8,128)(2,1)} %convolution_convert_fusion), kind=kCustom, calls=%all-reduce-scatter | all-reduce-scatter fusion | flops 6553601 | bytes 11060224
  639.3 2.0 collective-permute-start.8
  641.3 6.0 collective-permute-start.7
  648.4 4.3 collective-permute-start.9
  652.8 8.8 collective-permute-done.9
  661.6 42.5 %collective-permute-start.6 = (bf16[64,3200]{1,0:T(8,128)(2,1)}, bf16[64,3200]{1,0:T(8,128)(2,1)}, u32[]{:S(2)}, u32[]{:S(2)}) collective-permute-start(bf16[64,3200]{1,0:T(8,128)(2,1)} %fusion), channel_id=1, source_target_pairs={{0,24},{8,32},{16,40},{24,48},{32,56},{40,64},{48,72},{56,80},{64,... | collective-permute-start | bytes 1228808
  704.1 34.7 %collective-permute-start.5 = (bf16[64,3200]{1,0:T(8,128)(2,1)}, bf16[64,3200]{1,0:T(8,128)(2,1)}, u32[]{:S(2)}, u32[]{:S(2)}) collective-permute-start(bf16[64,3200]{1,0:T(8,128)(2,1)} %fusion), channel_id=1, source_target_pairs={{0,16},{8,24},{16,32},{24,40},{32,48},{40,56},{48,64},{56,72},{64,... | collective-permute-start | bytes 1228808
  738.8 1.9 collective-permute-start.4
  742.0 2.4 collective-permute-done.5
  744.4 7.9 collective-permute-done.4
  752.3 27.9 %concatenate.19 = bf16[436,3200]{1,0:T(8,128)(2,1)} concatenate(bf16[52,3200]{1,0:T(8,128)(2,1)} %collective-permute-done.9, bf16[64,3200]{1,0:T(8,128)(2,1)} %collective-permute-done.8, bf16[64,3200]{1,0:T(8,128)(2,1)} %collective-permute-done.7, bf16[64,3200]{1,0:T(8,128)(2,1)} %collective-permute-done.6, bf16[64,3200]{1,0:T(8,128)(2,1)} %collective-permute-done.5, ...), dimensions={0} | concatenate | bytes 5580800
  780.2 1.9 dynamic-slice_convert_fusion
  782.1 2.8 copy.87
  785.0 5.2 multiply_convert_fusion
  790.1 2.2 copy.67
  792.3 8.8 fusion.10
  801.1 76.3 %reduce-scatter.6.cloned.1.call-done = f32[400,52]{1,0:T(8,128)} async-done(((f32[3200,52]{1,0:T(8,128)}), f32[400,52]{1,0:T(8,128)}) %reduce-scatter.6.cloned.1.call-update) | async-done | bytes 83216
  877.4 1.7 copy.88
  879.1 4.3 fusion.12
  883.5 1.4 copy.69
  884.9 1.3 copy.68
  (46 shorter events, 9.5 us)
Async XLA Ops:
  7.2 118.8 %copy-start = (bf16[1,256,3200]{2,1,0:T(8,128)(2,1)S(1)}, bf16[1,256,3200]{2,1,0:T(8,128)(2,1)}, u32[]{:S(2)}) copy-start(bf16[1,256,3200]{2,1,0:T(8,128)(2,1)} %param.13) | copy-start | bytes 4915204
  7.2 10.6 %copy-start.10 = (s32[1,32]{1,0:T(1,128)S(1)}, s32[1,32]{1,0:T(1,128)}, u32[]{:S(2)}) copy-start(s32[1,32]{1,0:T(1,128)} %param.15) | copy-start | bytes 388
  7.2 118.8 %all-gather.2.cloned.1.call-start = ((), (), s32[]{:S(2)}) async-start(), calls=%async_computation.1 | async-start | bytes 11980800 | tf_op jit(solution)/shard_map/all_gather | solution.py:101
  7.9 869.4 %reduce-scatter.6.cloned.1.call-start = ((), (), s32[]{:S(2)}) async-start(), calls=%async_computation.2 | async-start | bytes 1843200
  11.1 130.3 %copy-start.5 = (bf16[1,256,1664]{1,2,0:T(8,128)(2,1)}, bf16[1,256,1664]{1,2,0:T(8,128)(2,1)S(1)}, u32[]{:S(2)}) copy-start(bf16[1,256,1664]{1,2,0:T(8,128)(2,1)S(1)} %copy.50) | copy-start | bytes 2555908
  12.5 40.3 %collective-permute-start.1 = (bf16[2,256,1664]{1,2,0:T(8,128)(2,1)}, bf16[2,256,1664]{1,2,0:T(8,128)(2,1)}, u32[]{:S(2)}, u32[]{:S(2)}) collective-permute-start(bf16[2,256,1664]{1,2,0:T(8,128)(2,1)} %pad_maximum_fusion.2), channel_id=1, source_target_pairs={{8,0},{16,8},{24,16},{32,24},{40,32},{48,40},{56,48},{64,56},{72,6... | collective-permute-start | bytes 5111816 | tf_op jit(solution)/shard_map/ppermute | solution.py:18
  14.7 41.9 %collective-permute-start = (bf16[2,256,1664]{1,2,0:T(8,128)(2,1)}, bf16[2,256,1664]{1,2,0:T(8,128)(2,1)}, u32[]{:S(2)}, u32[]{:S(2)}) collective-permute-start(bf16[2,256,1664]{1,2,0:T(8,128)(2,1)} %pad_maximum_fusion.2), channel_id=1, source_target_pairs={{0,8},{8,16},{16,24},{24,32},{32,40},{40,48},{48,56},{56,64},{64,7... | collective-permute-start | bytes 5111816 | tf_op jit(solution)/shard_map/ppermute | solution.py:15
  65.0 3.7 copy-start.1
  135.7 5.7 copy-start.6
  135.7 7.2 copy-start.2
  135.7 7.3 copy-start.8
  135.7 7.6 copy-start.9
  153.3 3.7 copy-start.4
  162.3 80.2 %copy-start.3 = (f32[1,256,13,128]{1,3,2,0:T(8,128)S(1)}, f32[1,256,13,128]{1,3,2,0:T(8,128)}, u32[]{:S(2)}) copy-start(f32[1,256,13,128]{1,3,2,0:T(8,128)} %get-tuple-element.121) | copy-start | bytes 5111812
  166.6 79.8 %copy-start.7 = (bf16[13,128,256]{2,1,0:T(8,128)(2,1)S(1)}, bf16[13,128,256]{2,1,0:T(8,128)(2,1)}, u32[]{:S(2)}) copy-start(bf16[13,128,256]{2,1,0:T(8,128)(2,1)} %get-tuple-element.119) | copy-start | bytes 2555908
  166.6 712.4 %collective-permute-start.2 = (f32[2,256,13,128]{1,3,2,0:T(8,128)}, f32[2,256,13,128]{1,3,2,0:T(8,128)}, u32[]{:S(2)}, u32[]{:S(2)}) collective-permute-start(f32[2,256,13,128]{1,3,2,0:T(8,128)} %pad_maximum_fusion), channel_id=1, source_target_pairs={{0,8},{8,16},{16,24},{24,32},{32,40},{40,48},{48,56},{56,64},{64,7... | collective-permute-start | bytes 10223624 | tf_op jit(solution)/shard_map/ppermute | solution.py:26
  244.5 634.5 %collective-permute-start.3 = (f32[2,256,13,128]{1,3,2,0:T(8,128)}, f32[2,256,13,128]{1,3,2,0:T(8,128)}, u32[]{:S(2)}, u32[]{:S(2)}) collective-permute-start(f32[2,256,13,128]{1,3,2,0:T(8,128)} %pad_maximum_fusion.1), channel_id=1, source_target_pairs={{8,0},{16,8},{24,16},{32,24},{40,32},{48,40},{56,48},{64,56},{72,6... | collective-permute-start | bytes 10223624 | tf_op jit(solution)/shard_map/ppermute | solution.py:26
  252.0 488.7 %copy-start.11 = (u32[256]{0:T(256)S(1)}, u32[256]{0:T(256)}, u32[]{:S(2)}) copy-start(u32[256]{0:T(256)} %constant.134) | copy-start | bytes 3076
  639.3 64.8 %collective-permute-start.8 = (bf16[64,3200]{1,0:T(8,128)(2,1)}, bf16[64,3200]{1,0:T(8,128)(2,1)}, u32[]{:S(2)}, u32[]{:S(2)}) collective-permute-start(bf16[64,3200]{1,0:T(8,128)(2,1)} %fusion), channel_id=1, source_target_pairs={{0,40},{8,48},{16,56},{24,64},{32,72},{40,80},{48,88},{56,96},{64,... | collective-permute-start | bytes 1228808
  641.3 97.5 %collective-permute-start.7 = (bf16[64,3200]{1,0:T(8,128)(2,1)}, bf16[64,3200]{1,0:T(8,128)(2,1)}, u32[]{:S(2)}, u32[]{:S(2)}) collective-permute-start(bf16[64,3200]{1,0:T(8,128)(2,1)} %fusion), channel_id=1, source_target_pairs={{0,32},{8,40},{16,48},{24,56},{32,64},{40,72},{48,80},{56,88},{64,... | collective-permute-start | bytes 1228808
  648.4 13.2 %collective-permute-start.9 = (bf16[52,3200]{1,0:T(8,128)(2,1)S(1)}, bf16[52,3200]{1,0:T(8,128)(2,1)}, u32[]{:S(2)}, u32[]{:S(2)}) collective-permute-start(bf16[52,3200]{1,0:T(8,128)(2,1)S(1)} %slice.196), channel_id=1, source_target_pairs={{0,48},{8,56},{16,64},{24,72},{32,80},{40,88},{48,96},{56,104},{64... | collective-permute-start | bytes 998408
  661.6 80.4 %collective-permute-start.6 = (bf16[64,3200]{1,0:T(8,128)(2,1)}, bf16[64,3200]{1,0:T(8,128)(2,1)}, u32[]{:S(2)}, u32[]{:S(2)}) collective-permute-start(bf16[64,3200]{1,0:T(8,128)(2,1)} %fusion), channel_id=1, source_target_pairs={{0,24},{8,32},{16,40},{24,48},{32,56},{40,64},{48,72},{56,80},{64,... | collective-permute-start | bytes 1228808
  704.1 40.3 %collective-permute-start.5 = (bf16[64,3200]{1,0:T(8,128)(2,1)}, bf16[64,3200]{1,0:T(8,128)(2,1)}, u32[]{:S(2)}, u32[]{:S(2)}) collective-permute-start(bf16[64,3200]{1,0:T(8,128)(2,1)} %fusion), channel_id=1, source_target_pairs={{0,16},{8,24},{16,32},{24,40},{32,48},{40,56},{48,64},{56,72},{64,... | collective-permute-start | bytes 1228808
  738.8 13.5 %collective-permute-start.4 = (bf16[64,3200]{1,0:T(8,128)(2,1)}, bf16[64,3200]{1,0:T(8,128)(2,1)}, u32[]{:S(2)}, u32[]{:S(2)}) collective-permute-start(bf16[64,3200]{1,0:T(8,128)(2,1)} %fusion), channel_id=1, source_target_pairs={{0,8},{8,16},{16,24},{24,32},{32,40},{40,48},{48,56},{56,64},{64,7... | collective-permute-start | bytes 1228808
Sparse Core Ops, SparseCore 0:
  9.8 116.1 all-gather.1
  785.1 92.2 reduce-scatter.5
where the time goes:
time: 901 us; the launch traced here: 893 us
  blocking collectives  387 us (43%)
  waiting for transfers between devices  183 us (20%)
  starting transfers between devices  175 us (19%)
  local copies, waits for them, and re-layouts  63.2 us (7%)
  matrix products  51.6 us (6%)
  other arithmetic  17.8 us (2%)
  between operations  15 us (2%)
    unnamed x1, blocking collectives  387 us
    unnamed x9, waiting for transfers between devices  96.1 us
    unnamed x7, starting transfers between devices  91.6 us
    ppermute x2, starting transfers between devices, passed_along(): return lax.ppermute(block, axis, route)  77.9 us
    all_gather x1, waiting for transfers between devices, on_device(): full_weight = lax.all_gather(out_weight, 'dp', axis=1, tiled=True)  57.2 us
    unnamed x35, local copies, waits for them, and re-layouts  47.7 us
    ppermute x1, waiting for transfers between devices, padded_2(): lax.ppermute(lax.slice_in_dim(block, 0, width, axis=dim), axis, backward)  30 us
  transfers between devices with their start and end apart: 12, of which 6 were waited for; matrix products, arithmetic and copies ran while one was open for 53% of the time, Pallas kernels for 0%

commit v1 on v0

v1 whole, which is shorter than its diff:
```python
import functools
import math

import jax
import jax.numpy as jnp
from jax import lax
from jax.experimental import pallas as pl
from jax.experimental.pallas import tpu as pltpu
from jax.sharding import PartitionSpec as P

HS = 128
ROWS = 256
HD = 1664
HEADS = 13
BLOCK = 400
PIECE = 96
REST = 16
GROUPS = ((0, 4), (4, 7), (7, 10), (10, 13))
MESH = pl.DeviceIdType.MESH
F32 = jnp.float32
BF16 = jnp.bfloat16
SCALE = HS ** (-0.5)
SCALE2 = SCALE * math.log2(math.e)


class Copies:
    def __init__(self, send, recv):
        self.send, self.recv, self.count = send, recv, 0
        self.started = []

    def start(self, src, dst, device):
        copy = pltpu.make_async_remote_copy(
            src_ref=src,
            dst_ref=dst,
            send_sem=self.send.at[self.count],
            recv_sem=self.recv.at[self.count],
            device_id=device,
            device_id_type=MESH,
        )
        self.count += 1
        copy.start()
        self.started.append(copy)
        return copy


def nt(a, b):
    return lax.dot_general(a, b, (((1,), (1,)), ((), ())), preferred_element_type=F32)


def tn(a, b):
    return lax.dot_general(a, b, (((0,), (0,)), ((), ())), preferred_element_type=F32)


def nn(a, b):
    return lax.dot_general(a, b, (((1,), (0,)), ((), ())), preferred_element_type=F32)


N_COPIES = 79


def body(
    q, k, v, go, wt, bias,
    res, dq, dk, dv, gw,
    kw, vw, w, probs, mx, gm, gop, dsend, drecv, down, term, yr1, yr2, ysum, xs, xr, zs, zr,
    local, send, recv,
):
    tm = lax.axis_index("tm")
    dp = lax.axis_index("dp")
    x, zh, y = tm % 4, (tm // 4) % 2, tm // 8
    zl, c = dp // 2, dp % 2
    z = zh * 4 + zl

    def place(x_, y_, z_, c_):
        return ((y_ * 2 + z_ // 4) * 4 + x_, (z_ % 4) * 2 + c_)

    up = (lax.rem(tm + 1, 32), dp)
    down_dev = (lax.rem(tm + 31, 32), dp)
    peer = place(x, y, z, 1 - c)
    along_x = [place(lax.rem(x + d, 4), y, z, c) for d in (1, 2, 3)]
    along_y = [place(x, lax.rem(y + d, 4), z, c) for d in (1, 2, 3)]
    along_z = [place(x, y, lax.rem(z + d, 8), c) for d in range(1, 8)]
    partners = [up, down_dev, peer] + along_x + along_y + along_z

    barrier = pltpu.get_barrier_semaphore()
    for device in partners:
        pl.semaphore_signal(barrier, inc=1, device_id=device, device_id_type=MESH)

    own_k = pltpu.make_async_copy(k, kw.at[pl.ds(ROWS, ROWS)], local.at[0])
    own_v = pltpu.make_async_copy(v, vw.at[pl.ds(ROWS, ROWS)], local.at[1])
    own_block = pl.multiple_of(zl * BLOCK, 16)
    own_w = pltpu.make_async_copy(wt, w.at[c, pl.ds(own_block, BLOCK)], local.at[2])
    own_k.start()
    own_v.start()
    own_w.start()
    for i in range(2):
        w[i, pl.ds(4 * BLOCK, HD - 4 * BLOCK), :] = jnp.zeros((HD - 4 * BLOCK, HD), BF16)

    copies = Copies(send, recv)
    pl.semaphore_wait(barrier, len(partners))

    def piece_at(block, at):
        return pl.ds(pl.multiple_of(block * BLOCK + at * PIECE, 16), PIECE)

    def rest_at(block):
        return pl.ds(pl.multiple_of(block * BLOCK + 4 * PIECE, 16), REST)

    w_z = []
    second = place(x, y, lax.rem(z + 2 + 4 * c, 8), c)
    for device in (along_z[0], along_z[6], second):
        w_z.append(copies.start(
            wt.at[pl.ds(pl.multiple_of(y * PIECE, 16), PIECE)], w.at[c, piece_at(zl, y)], device))
        w_z.append(copies.start(wt.at[pl.ds(4 * PIECE, REST)], w.at[c, rest_at(zl)], device))

    halo = []
    for first, last in GROUPS:
        lanes = pl.ds(first * HS, (last - first) * HS)
        group = []
        for src, dst in ((k, kw), (v, vw)):
            group.append(copies.start(src.at[:, lanes], dst.at[pl.ds(0, ROWS), lanes], up))
            group.append(copies.start(src.at[:, lanes], dst.at[pl.ds(2 * ROWS, ROWS), lanes], down_dev))
        halo.append(group)
    w_peer = [copies.start(wt, w.at[c, pl.ds(own_block, BLOCK)], peer)]
    go_peer = copies.start(go.at[1 - c], gop, peer)

    others = [lax.rem(zl + d, 4) for d in (1, 2, 3)]
    for copy in w_z:
        copy.wait_recv()
    w_y = []
    for device in along_y:
        for block in others:
            at = piece_at(block, y)
            w_y.append(copies.start(w.at[c, at], w.at[c, at], device))
    for block in others:
        for at in (piece_at(block, y), rest_at(block)):
            w_peer.append(copies.start(w.at[c, at], w.at[c, at], peer))

    own_k.wait()
    own_v.wait()
    own_w.wait()

    def forward(h, carry):
        lanes = pl.ds(pl.multiple_of(h * HS, HS), HS)
        s = nt(q[:, lanes], kw[:, lanes]) * SCALE2 + bias[...]
        e = jnp.exp2(s - jnp.max(s, axis=-1, keepdims=True))
        p = (e * (1.0 / jnp.sum(e, axis=-1, keepdims=True))).astype(BF16)
        probs[h] = p
        mx[0, :, lanes] = nn(p, vw[:, lanes]).astype(BF16)
        return carry

    def w_along_y():
        for i, d in enumerate((1, 2, 3)):
            for j, block in enumerate(others):
                w_y[3 * i + j].wait_recv()
                at = piece_at(block, lax.rem(y + 4 - d, 4))
                w_peer.append(copies.start(w.at[c, at], w.at[c, at], peer))

    for index, (first, last) in enumerate(GROUPS):
        if index == 3:
            w_along_y()
        for copy in halo[index]:
            copy.wait_recv()
        lax.fori_loop(first, last, forward, 0)
    mx_peer = copies.start(mx.at[0], mx.at[1], peer)

    for copy in w_peer:
        copy.wait_recv()

    def backward(h, carry):
        lanes = pl.ds(pl.multiple_of(h * HS, HS), HS)
        g = gm[:, lanes]
        p = probs[h]
        delta = jnp.sum(g.astype(F32) * mx[0, :, lanes].astype(F32), axis=-1, keepdims=True)
        ds = (p.astype(F32) * (nt(g, vw[:, lanes]) - delta)).astype(BF16)
        dq[:, lanes] = (nn(ds, kw[:, lanes]) * SCALE).astype(BF16)
        for which, grad in ((0, tn(ds, q[:, lanes]) * SCALE), (1, tn(p, g))):
            dsend[0, which, :, lanes] = grad[:ROWS].astype(BF16)
            down[which, :, lanes] = grad[ROWS : 2 * ROWS]
            dsend[1, which, :, lanes] = grad[2 * ROWS :].astype(BF16)
        return carry

    grads = []
    for first, last in GROUPS:
        lanes = pl.ds(first * HS, (last - first) * HS)
        gm[:, lanes] = (nn(go[0], w[0, :, lanes]) + nn(go[1], w[1, :, lanes])).astype(BF16)
        lax.fori_loop(first, last, backward, 0)
        group = []
        for which in (0, 1):
            group.append(copies.start(dsend.at[0, which, :, lanes], drecv.at[0, which, :, lanes], down_dev))
            group.append(copies.start(dsend.at[1, which, :, lanes], drecv.at[1, which, :, lanes], up))
        grads.append(group)

    go_peer.wait_recv()
    mx_peer.wait_recv()

    def weight_term(h, carry):
        lanes = pl.ds(pl.multiple_of(h * HS, HS), HS)
        term[lanes, :] = (tn(mx[0, :, lanes], go[c]) + tn(mx[1, :, lanes], gop[...])).astype(BF16)
        return carry

    lax.fori_loop(0, HEADS, weight_term, 0)

    def chunk(at, half=None):
        if half is None:
            return pl.ds(pl.multiple_of(at * 416, 16), 416)
        return pl.ds(pl.multiple_of(at * 416 + half * 208, 16), 208)

    after, across, before = [lax.rem(y + d, 4) for d in (1, 2, 3)]
    y_first = [
        copies.start(term.at[chunk(across, 0)], yr1.at[0], along_y[0]),
        copies.start(term.at[chunk(across, 1)], yr1.at[1], along_y[2]),
    ]

    def project(i):
        for at, size in ((0, 640), (640, 512), (1152, 512)):
            res[i, :, at : at + size] = nt(mx[0], w[i, at : at + size, :]).astype(BF16)

    project(0)
    y_second = []
    for half, target, device in ((0, after, along_y[0]), (1, before, along_y[2])):
        y_first[half].wait_recv()
        term[chunk(target, half), :] = (
            term[chunk(target, half), :].astype(F32) + yr1[half].astype(F32)
        ).astype(BF16)
        y_second.append(copies.start(term.at[chunk(target)], yr2.at[half], device))
    project(1)
    for copy in y_second:
        copy.wait_recv()
    ysum[pl.ds(416, 16), :] = jnp.zeros((16, HD), F32)
    ysum[pl.ds(0, 416), :] = (
        term[chunk(y), :].astype(F32) + yr2[0].astype(F32) + yr2[1].astype(F32)
    )
    for to in range(4):
        for half in range(2):
            xs[to, half] = ysum[pl.ds(208 * half + 52 * to, 64), :].astype(BF16)
    x_copies = [
        copies.start(xs.at[lax.rem(x + d, 4)], xr.at[d - 1], along_x[d - 1]) for d in (1, 2, 3)
    ]
    for copy in x_copies:
        copy.wait_recv()
    for half in range(2):
        total = xs[x, half].astype(F32)
        for i in range(3):
            total = total + xr[i, half].astype(F32)
        for block in range(4):
            turned = total if block == 0 else pltpu.roll(total, HD - BLOCK * block, 1)
            zs[half * 4 + block] = turned[:, :512].astype(BF16)
    z_copies = [
        copies.start(zs.at[lax.rem(z + d, 8)], zr.at[d - 1], along_z[d - 1]) for d in range(1, 8)
    ]
    for copy in z_copies:
        copy.wait_recv()
    total = zs[z].astype(F32)
    for i in range(7):
        total = total + zr[i].astype(F32)
    gw[...] = total.astype(BF16)

    for (first, last), group in zip(GROUPS, grads):
        lanes = pl.ds(first * HS, (last - first) * HS)
        for copy in group:
            copy.wait_recv()
        for which, out in ((0, dk), (1, dv)):
            out[:, lanes] = (
                down[which, :, lanes]
                + drecv[0, which, :, lanes].astype(F32)
                + drecv[1, which, :, lanes].astype(F32)
            ).astype(BF16)
    for copy in copies.started:
        copy.wait_send()


def on_device(queries, keys, values, grad_out, out_weight, frame_clip):
    tm = lax.axis_index("tm")
    extended = jnp.pad(frame_clip[0], 1, constant_values=-1)
    near = lax.dynamic_slice_in_dim(extended, tm, 3)
    bias = jnp.repeat(jnp.where(near == near[1], 0.0, -1e30).astype(F32), ROWS)[None]
    go = grad_out[0].reshape(ROWS, 4, 2, BLOCK).transpose(2, 0, 1, 3).reshape(2, ROWS, 4 * BLOCK)
    go = jnp.pad(go, ((0, 0), (0, 0), (0, HD - 4 * BLOCK)))
    vmem = pl.BlockSpec(memory_space=pltpu.VMEM)
    hbm = pl.BlockSpec(memory_space=pl.ANY)
    half = jax.ShapeDtypeStruct((ROWS, HD), BF16)
    res, dq, dk, dv, gw = pl.pallas_call(
        body,
        out_shape=(
            jax.ShapeDtypeStruct((2, ROWS, HD), BF16),
            half,
            half,
            half,
            jax.ShapeDtypeStruct((64, 512), BF16),
        ),
        in_specs=[vmem, hbm, hbm, vmem, vmem, vmem],
        out_specs=(vmem,) * 5,
        scratch_shapes=[
            pltpu.VMEM((3 * ROWS, HD), BF16),
            pltpu.VMEM((3 * ROWS, HD), BF16),
            pltpu.VMEM((2, HD, HD), BF16),
            pltpu.VMEM((HEADS, ROWS, 3 * ROWS), BF16),
            pltpu.VMEM((2, ROWS, HD), BF16),
            pltpu.VMEM((ROWS, HD), BF16),
            pltpu.VMEM((ROWS, HD), BF16),
            pltpu.VMEM((2, 2, ROWS, HD), BF16),
            pltpu.VMEM((2, 2, ROWS, HD), BF16),
            pltpu.VMEM((2, ROWS, HD), F32),
            pltpu.VMEM((HD, HD), BF16),
            pltpu.VMEM((2, 208, HD), BF16),
            pltpu.VMEM((2, 416, HD), BF16),
            pltpu.VMEM((432, HD), F32),
            pltpu.VMEM((4, 2, 64, HD), BF16),
            pltpu.VMEM((3, 2, 64, HD), BF16),
            pltpu.VMEM((8, 64, 512), BF16),
            pltpu.VMEM((7, 64, 512), BF16),
            pltpu.SemaphoreType.DMA((3,)),
            pltpu.SemaphoreType.DMA((N_COPIES,)),
            pltpu.SemaphoreType.DMA((N_COPIES,)),
        ],
        compiler_params=pltpu.CompilerParams(
            collective_id=0, has_side_effects=True, vmem_limit_bytes=63 * 1024 * 1024
        ),
        cost_estimate=pl.CostEstimate(flops=12_100_000_000, bytes_accessed=25_000_000, transcendentals=2_600_000),
        name="attention_and_projection",
    )(queries[0], keys[0], values[0], go, out_weight.T, bias)
    result = res[:, :, : 4 * BLOCK].reshape(2, ROWS, 4, BLOCK).transpose(1, 2, 0, 3)
    return (
        result.reshape(1, ROWS, 8 * BLOCK),
        dq[None],
        dk[None],
        dv[None],
        gw[:52, :BLOCK],
    )


def solution(mesh):
    in_specs = (
        P("dp", "tm", None),
        P("dp", "tm", None),
        P("dp", "tm", None),
        P("dp", "tm", None),
        P(None, "dp"),
        P("dp", None),
    )
    out_specs = (
        P("dp", "tm", None),
        P("dp", "tm", None),
        P("dp", "tm", None),
        P("dp", "tm", None),
        P("tm", "dp"),
    )
    return jax.shard_map(
        on_device, mesh=mesh, in_specs=in_specs, out_specs=out_specs, check_vma=False
    )
```

time: 901 us -> 290 us (0.32)
  blocking collectives: 387 us -> 0 us
  Pallas kernels: 0 us -> 267 us
  waiting for transfers between devices: 183 us -> 0 us
  starting transfers between devices: 175 us -> 0 us
  matrix products: 51.6 us -> 0 us
  local copies, waits for them, and re-layouts: 63.2 us -> 16.3 us
  other arithmetic: 17.8 us -> 1.38 us
  between operations: 15 us -> 0.71 us
    unnamed x1 -> x0, blocking collectives: 387 us -> none
    pallas_call x0 -> x1, Pallas kernels: none -> 267 us  [on_device(): pl.pallas_call(body, out_shape=(jax.ShapeDtypeStruct((2, ROWS, HD), BF16)...]
    unnamed x9 -> x0, waiting for transfers between devices: 96.1 us -> none
    unnamed x7 -> x0, starting transfers between devices: 91.6 us -> none
    ppermute x4 -> x0, starting transfers between devices: 83.1 us -> none  [the longest x2 77.9 us: passed_along(): return lax.ppermute(block, axis, route)]
    all_gather x1 -> x0, waiting for transfers between devices: 57.2 us -> none  [on_device(): full_weight = lax.all_gather(out_weight, 'dp', axis=1, tiled=True)]
    dot_general x9 -> x0, matrix products: 51.6 us -> none  [the longest x1 8.75 us: on_device(): jnp.dot(mixed_rows, full_weight, preferred_element_type=jnp.float32)]
    unnamed x35 -> x15, local copies, waits for them, and re-layouts: 47.7 us -> 8.7 us
  transfers between devices with their start and end apart: 12 -> 0, of which waited for: 6 -> 0; matrix products, arithmetic and copies ran while one was open for 53% -> 0% of each run, Pallas kernels for 0% -> 0%
where the time goes in v1:
time: 290 us; the launch traced here: 285 us
  Pallas kernels  267 us (92%)
  local copies, waits for them, and re-layouts  16.3 us (6%)
    pallas_call x1, Pallas kernels, on_device(): pl.pallas_call(body, out_shape=(jax.ShapeDtypeStruct((2, ROWS, HD), BF16)...  267 us
    unnamed x15, local copies, waits for them, and re-layouts  8.7 us

profile of v1, /device:TPU:37, one launch (start us, length us, event | category | flops | bytes accessed | tf_op | source)
XLA Modules:
  0.0 285.2 jit_solution(8684907096890339334)
XLA Ops:
  0.6 0.7 pad_dynamic-slice_fusion
  1.4 0.6 slice.9
  2.0 1.4 compare_select_fusion
  3.3 0.1 broadcast_bitcast_fusion
  3.4 0.6 copy.19
  4.0 3.0 %copy.13 = bf16[1,256,3200]{1,2,0:T(8,128)(2,1)S(1)} copy(bf16[1,256,3200]{2,1,0:T(8,128)(2,1)} %param.9) | data formatting | bytes 3276800 | tf_op args[3]
  7.0 0.1 copy.14
  7.1 1.4 copy.15
  8.5 1.3 pad.8.go
  9.8 266.8 %attention_and_projection.1 = (bf16[2,256,1664]{2,1,0:T(8,128)(2,1)}, bf16[256,1664]{1,0:T(8,128)(2,1)}, bf16[256,1664]{1,0:T(8,128)(2,1)}, bf16[256,1664]{1,0:T(8,128)(2,1)}, bf16[64,512]{1,0:T(8,128)(2,1)}) custom-call(bf16[256,1664]{1,0:T(8,128)(2,1)} %bitcast.34, bf16[256,1664]{1,0:T(8,128)(2,1)} %bitcast.35, bf16[256,1664]{1,0:T(8,128)(2,1)} %bitcast.36, ...), custom_call_target="tpu_custom_call" | custom-call | flops 12099999744 | bytes 25000000 | tf_op jit(solution)/shard_map/attention_and_projection/pallas_call | solution.py:281
  276.6 2.8 copy.16
  279.4 0.1 copy.17
  279.5 0.0 copy-start.3
  279.5 0.0 copy-start.2
  279.5 2.3 copy.18
  281.9 0.0 copy-start.1
  281.9 0.0 copy-done.3
  281.9 0.6 slice.11
  282.5 0.0 copy-done.2
  282.5 0.0 copy-start
  282.5 0.9 copy.23
  283.4 0.0 copy-done.1
  283.4 0.9 copy.24
  284.3 0.0 copy-done
  284.3 0.9 copy.25
Async XLA Ops:
  279.5 2.4 copy-start.3
  279.5 3.0 %copy-start.2 = (bf16[256,1664]{1,0:T(8,128)(2,1)S(1)}, bf16[256,1664]{1,0:T(8,128)(2,1)}, u32[]{:S(2)}) copy-start(bf16[256,1664]{1,0:T(8,128)(2,1)} %get-tuple-element.11) | copy-start | bytes 2555908
  281.9 1.5 copy-start.1
  282.5 1.8 copy-start

commit v2 on v1

v2 whole, which is shorter than its diff:
```python
import functools
import math

import jax
import jax.numpy as jnp
from jax import lax
from jax.experimental import pallas as pl
from jax.experimental.pallas import tpu as pltpu
from jax.sharding import PartitionSpec as P

HS = 128
ROWS = 256
HD = 1664
HEADS = 13
BLOCK = 400
PIECE = 96
REST = 16
GROUPS = ((0, 3), (3, 6), (6, 9), (9, 11), (11, 13))
ORDER = (3, 4, 0, 1, 2)
HALF = 896
WIDE = 1664
MESH = pl.DeviceIdType.MESH
F32 = jnp.float32
BF16 = jnp.bfloat16
SCALE = HS ** (-0.5)
SCALE2 = SCALE * math.log2(math.e)


class Copies:
    def __init__(self, send, recv):
        self.send, self.recv, self.count = send, recv, 0
        self.started = []

    def start(self, src, dst, device):
        copy = pltpu.make_async_remote_copy(
            src_ref=src,
            dst_ref=dst,
            send_sem=self.send.at[self.count],
            recv_sem=self.recv.at[self.count],
            device_id=device,
            device_id_type=MESH,
        )
        self.count += 1
        copy.start()
        self.started.append(copy)
        return copy


def nt(a, b):
    return lax.dot_general(a, b, (((1,), (1,)), ((), ())), preferred_element_type=F32)


def tn(a, b):
    return lax.dot_general(a, b, (((0,), (0,)), ((), ())), preferred_element_type=F32)


def nn(a, b):
    return lax.dot_general(a, b, (((1,), (0,)), ((), ())), preferred_element_type=F32)


N_COPIES = 47


class Beside:
    def __init__(self, x, up, down, mid_up, mid_down, over_up, over_down, to_up, to_down, held, sems):
        self.x, self.up, self.down = x, up, down
        self.mid_up, self.mid_down = mid_up, mid_down
        self.over_up, self.over_down = over_up, over_down
        self.to_up, self.to_down, self.held = to_up, to_down, held
        self.send, self.recv, self.in_send, self.in_recv, self.on_send = sems

    def direct(self, group, which, way):
        first, last = GROUPS[group]
        lanes = pl.ds(first * HS, (last - first) * HS)
        src, dst = (self.to_up, self.to_down)[way](which, lanes)
        at = (group * 2 + which) * 2 + way
        return pltpu.make_async_remote_copy(
            src_ref=src, dst_ref=dst, send_sem=self.send.at[at], recv_sem=self.recv.at[at],
            device_id=(self.up, self.down)[way], device_id_type=MESH,
        )

    def into(self, group, which, way):
        first, last = GROUPS[group]
        lanes = pl.ds(first * HS, (last - first) * HS)
        src, _ = (self.to_up, self.to_down)[way](which, lanes)
        at = way * 2 + which
        return pltpu.make_async_remote_copy(
            src_ref=src, dst_ref=self.held.at[way, which], send_sem=self.in_send.at[at], recv_sem=self.in_recv.at[at],
            device_id=(self.mid_up, self.mid_down)[way][group - 3], device_id_type=MESH,
        )

    def onward(self, group, which, way):
        first, last = GROUPS[group]
        lanes = pl.ds(first * HS, (last - first) * HS)
        _, dst = (self.to_up, self.to_down)[way](which, lanes)
        return pltpu.make_async_remote_copy(
            src_ref=self.held.at[way, which], dst_ref=dst, send_sem=self.on_send.at[way * 2 + which],
            recv_sem=self.recv.at[(group * 2 + which) * 2 + way],
            device_id=(self.over_up, self.over_down)[way], device_id_type=MESH,
        )

    def inner(self, way):
        return self.x != (3, 0)[way]

    def start_inner(self, groups):
        for way in (0, 1):
            @pl.when(self.inner(way))
            def _():
                for group in groups:
                    for which in (0, 1):
                        self.direct(group, which, way).start()

    def start_into(self, group):
        for way in (0, 1):
            @pl.when(jnp.logical_not(self.inner(way)))
            def _():
                for which in (0, 1):
                    self.into(group, which, way).start()

    def start_over(self, groups):
        for way in (0, 1):
            @pl.when(jnp.logical_not(self.inner(way)))
            def _():
                for group in groups:
                    for which in (0, 1):
                        self.direct(group, which, way).start()

    def pass_on(self):
        for column in (1, 2):
            @pl.when(self.x == column)
            def _():
                for way in (0, 1):
                    group = 3 if (way == 0) == (column == 2) else 4
                    for which in (0, 1):
                        self.into(group, which, way).wait_recv()
                        self.onward(group, which, way).start()

    def wait(self, group):
        for way in (0, 1):
            for which in (0, 1):
                self.direct(group, which, way).wait_recv()

    def drain(self):
        for way in (0, 1):
            for which in (0, 1):
                for group in range(3):
                    self.direct(group, which, way).wait_send()

                @pl.when(self.inner(way))
                def _():
                    for group in (3, 4):
                        self.direct(group, which, way).wait_send()

                @pl.when(jnp.logical_not(self.inner(way)))
                def _():
                    for group in (3, 4):
                        self.into(group, which, way).wait_send()

                @pl.when(jnp.logical_or(self.x == 1, self.x == 2))
                def _():
                    self.onward(3, which, way).wait_send()


def body(
    q, k, v, go, weight, clip,
    res, dq, dk, dv, gw,
    kw, vw, w, bias, probs, mx, gm, gop, dsend, drecv, down, held_kv, held_grad,
    term, yr1, yr2, ysum, xs, xr, zs, zr,
    local, send, recv, z_send, z_recv, *edge_sems,
):
    tm = lax.axis_index("tm")
    dp = lax.axis_index("dp")
    x, zh, y = tm % 4, (tm // 4) % 2, tm // 8
    zl, c = dp // 2, dp % 2
    z = zh * 4 + zl

    def place(x_, y_, z_, c_):
        return ((y_ * 2 + z_ // 4) * 4 + x_, (z_ % 4) * 2 + c_)

    def in_row(x_, step):
        return (lax.rem(tm // 4 + 8 + step, 8) * 4 + x_, dp)

    up = (lax.rem(tm + 1, 32), dp)
    down_dev = (lax.rem(tm + 31, 32), dp)
    peer = place(x, y, z, 1 - c)
    along_x = [place(lax.rem(x + d, 4), y, z, c) for d in (1, 2, 3)]
    along_y = [place(x, lax.rem(y + d, 4), z, c) for d in (1, 2, 3)]
    along_z = [place(x, y, lax.rem(z + d, 8), c) for d in range(1, 8)]
    across_z = [place(x, y, lax.rem(z + d, 8), 1 - c) for d in range(1, 8)]
    partners = [up, down_dev, peer] + along_x + along_y + along_z + across_z

    barrier = pltpu.get_barrier_semaphore()
    for device in partners:
        pl.semaphore_signal(barrier, inc=1, device_id=device, device_id_type=MESH)
    for column, step in ((0, -1), (3, 1)):
        @pl.when(x == column)
        def _():
            for column_ in (1, 2):
                pl.semaphore_signal(barrier, inc=1, device_id=in_row(column_, step), device_id_type=MESH)

    own_k = pltpu.make_async_copy(k, kw.at[pl.ds(ROWS, ROWS)], local.at[0])
    own_v = pltpu.make_async_copy(v, vw.at[pl.ds(ROWS, ROWS)], local.at[1])
    own_k.start()
    own_v.start()
    own = pl.ds(pl.multiple_of(dp * BLOCK, 16), BLOCK)
    for h in range(HEADS):
        w[own, h * HS : (h + 1) * HS] = weight[h * HS : (h + 1) * HS, :].T
    here = clip[0, tm]
    before_off = jnp.where(jnp.logical_and(tm > 0, clip[0, lax.rem(tm + 31, 32)] == here), 0.0, -1e30).astype(F32)
    after_off = jnp.where(jnp.logical_and(tm < 31, clip[0, lax.rem(tm + 1, 32)] == here), 0.0, -1e30).astype(F32)
    bias[:, pl.ds(0, ROWS)] = jnp.full((8, ROWS), before_off, F32)
    bias[:, pl.ds(ROWS, ROWS)] = jnp.zeros((8, ROWS), F32)
    bias[:, pl.ds(2 * ROWS, ROWS)] = jnp.full((8, ROWS), after_off, F32)

    copies = Copies(send, recv)
    mid = ((in_row(2, 0), in_row(1, 0)), (in_row(1, 0), in_row(2, 0)))
    over = (in_row(0, 1), in_row(3, -1))
    windows = (kw, vw)
    inputs = (k, v)
    keys_values = Beside(
        x, up, down_dev, *mid, *over,
        lambda which, lanes: (inputs[which].at[:, lanes], windows[which].at[pl.ds(0, ROWS), lanes]),
        lambda which, lanes: (inputs[which].at[:, lanes], windows[which].at[pl.ds(2 * ROWS, ROWS), lanes]),
        held_kv, edge_sems[:5],
    )
    grads = Beside(
        x, up, down_dev, *mid, *over,
        lambda which, lanes: (dsend.at[1, which, :, lanes], drecv.at[1, which, :, lanes]),
        lambda which, lanes: (dsend.at[0, which, :, lanes], drecv.at[0, which, :, lanes]),
        held_grad, edge_sems[5:],
    )
    pl.semaphore_wait(barrier, len(partners) + 2 * jnp.logical_or(x == 1, x == 2).astype(jnp.int32))

    def piece_at(block, at):
        return w.at[pl.ds(pl.multiple_of(block * BLOCK + at * PIECE, 16), PIECE)]

    def rest_at(block):
        return w.at[pl.ds(pl.multiple_of(block * BLOCK + 4 * PIECE, 16), REST)]

    def same(ref, device):
        return copies.start(ref, ref, device)

    w_z = []
    second = place(x, y, lax.rem(z + 2 + 4 * c, 8), c)
    for device in (along_z[0], along_z[6], second):
        w_z.append(same(piece_at(dp, y), device))
        w_z.append(same(rest_at(dp), device))
    for group in (3, 4):
        keys_values.start_into(group)
    keys_values.start_inner(ORDER)
    w_peer = [same(w.at[own], peer)]
    go_peer = copies.start(go.at[:, pl.ds(pl.multiple_of(1536 * (1 - c), 128), WIDE)], gop, peer)

    others = [lax.rem(zl + d, 4) * 2 + c for d in (1, 2, 3)]
    for copy in w_z:
        copy.wait_recv()
    w_y = []
    for device in along_y:
        for block in others:
            w_y.append(same(piece_at(block, y), device))
    keys_values.start_over((0, 1, 2))
    for block in others:
        w_peer.append(same(piece_at(block, y), peer))
        w_peer.append(same(rest_at(block), peer))
    keys_values.pass_on()

    own_k.wait()
    own_v.wait()

    def forward(h, carry):
        lanes = pl.ds(pl.multiple_of(h * HS, HS), HS)
        s = nt(q[:, lanes], kw[:, lanes]) * SCALE2 + bias[0:1, :]
        e = jnp.exp2(s - jnp.max(s, axis=-1, keepdims=True))
        p = (e * (1.0 / jnp.sum(e, axis=-1, keepdims=True))).astype(BF16)
        probs[h] = p
        mx[0, :, lanes] = nn(p, vw[:, lanes]).astype(BF16)
        return carry

    def w_along_y():
        for i, d in enumerate((1, 2, 3)):
            for j, block in enumerate(others):
                w_y[3 * i + j].wait_recv()
                w_peer.append(same(piece_at(block, lax.rem(y + 4 - d, 4)), peer))

    for index, group in enumerate(ORDER):
        if index == 4:
            w_along_y()
        keys_values.wait(group)
        lax.fori_loop(*GROUPS[group], forward, 0)
    mx_peer = copies.start(mx.at[0], mx.at[1], peer)

    go_peer.wait_recv()
    mx_peer.wait_recv()

    def chunk(p, at, half=None):
        if half is None:
            return term.at[p, pl.ds(pl.multiple_of(at * 416, 16), 416)]
        return term.at[p, pl.ds(pl.multiple_of(at * 416 + half * 208, 16), 208)]

    after, across, before = [lax.rem(y + d, 4) for d in (1, 2, 3)]
    y_first, y_second, x_copies = [], [], []
    for p in (0, 1):
        def weight_term(h, carry):
            lanes = pl.ds(pl.multiple_of(h * HS, HS), HS)
            columns = pl.ds(pl.multiple_of(1536 * c + 768 * p, 128), HALF)
            term[p, lanes, :] = (
                tn(mx[0, :, lanes], go[:, columns]) + tn(mx[1, :, lanes], gop[:, 768 * p : 768 * p + HALF])
            ).astype(BF16)
            return carry

        lax.fori_loop(0, HEADS, weight_term, 0)
        y_first.append([
            copies.start(chunk(p, across, 0), yr1.at[p, 0], along_y[0]),
            copies.start(chunk(p, across, 1), yr1.at[p, 1], along_y[2]),
        ])

    def y_next(p):
        pair = []
        for half, target, device in ((0, after, along_y[0]), (1, before, along_y[2])):
            y_first[p][half].wait_recv()
            part = chunk(p, target, half)
            part[...] = (part[...].astype(F32) + yr1[p, half].astype(F32)).astype(BF16)
            pair.append(copies.start(chunk(p, target), yr2.at[p, half], device))
        y_second.append(pair)

    for copy in w_peer:
        copy.wait_recv()

    def backward(h, carry):
        lanes = pl.ds(pl.multiple_of(h * HS, HS), HS)
        g = gm[:, lanes]
        p = probs[h]
        delta = jnp.sum(g.astype(F32) * mx[0, :, lanes].astype(F32), axis=-1, keepdims=True)
        ds = (p.astype(F32) * (nt(g, vw[:, lanes]) - delta)).astype(BF16)
        dq[:, lanes] = (nn(ds, kw[:, lanes]) * SCALE).astype(BF16)
        for which, grad in ((0, tn(ds, q[:, lanes]) * SCALE), (1, tn(p, g))):
            dsend[0, which, :, lanes] = grad[:ROWS].astype(BF16)
            down[which, :, lanes] = grad[ROWS : 2 * ROWS]
            dsend[1, which, :, lanes] = grad[2 * ROWS :].astype(BF16)
        return carry

    for index, group in enumerate(ORDER):
        first, last = GROUPS[group]
        lanes = pl.ds(first * HS, (last - first) * HS)
        gm[:, lanes] = nn(go[...], w[:, lanes]).astype(BF16)
        lax.fori_loop(first, last, backward, 0)
        if group > 2:
            grads.start_into(group)
        else:
            grads.start_over((group,))
        grads.start_inner((group,))
        if index in (1, 3):
            y_next(index // 2)

    for i in range(5):
        columns = pl.ds(i * 640, 640)
        res[:, columns] = nt(mx[0], w[columns, :]).astype(BF16)
    grads.pass_on()

    for p in (0, 1):
        for copy in y_second[p]:
            copy.wait_recv()
        ysum[pl.ds(0, 416), :] = (
            chunk(p, y)[...].astype(F32) + yr2[p, 0].astype(F32) + yr2[p, 1].astype(F32)
        )
        ysum[pl.ds(416, 16), :] = jnp.zeros((16, HALF), F32)
        for to in range(4):
            for half in range(2):
                xs[p, to, half] = ysum[pl.ds(208 * half + 52 * to, 64), :].astype(BF16)
        x_copies.append([
            copies.start(xs.at[p, lax.rem(x + d, 4)], xr.at[p, d - 1], along_x[d - 1]) for d in (1, 2, 3)
        ])

    def to_owner(p, half, b):
        at = p * 4 + half * 2 + b
        z_to = half * 4 + c * 2 + p
        slot = lax.rem(z + 8 - z_to, 8)
        mine = jnp.logical_and(z_to == z, c == b)
        return mine, at, pltpu.make_async_remote_copy(
            src_ref=zs.at[at], dst_ref=zr.at[slot], send_sem=z_send.at[at], recv_sem=z_recv.at[slot],
            device_id=place(x, y, z_to, b), device_id_type=MESH,
        )

    for p in (0, 1):
        for copy in x_copies[p]:
            copy.wait_recv()
        for half in range(2):
            total = xs[p, x, half].astype(F32)
            for i in range(3):
                total = total + xr[p, i, half].astype(F32)
            for b in (0, 1):
                shift = lax.rem(2 * HALF - BLOCK * b - 32 * p - 64 * c, HALF)
                zs[p * 4 + half * 2 + b] = pltpu.roll(total, shift, 1)[:, :512].astype(BF16)
        for half in range(2):
            for b in (0, 1):
                mine, at, copy = to_owner(p, half, b)

                @pl.when(mine)
                def _():
                    zr[0] = zs[at]

                @pl.when(jnp.logical_not(mine))
                def _():
                    copy.start()

    def from_z(slot):
        return pltpu.make_async_remote_copy(
            src_ref=zs.at[0], dst_ref=zr.at[slot], send_sem=z_send.at[0], recv_sem=z_recv.at[slot],
            device_id=peer, device_id_type=MESH,
        )

    for slot in range(1, 8):
        from_z(slot).wait_recv()

    @pl.when(zl // 2 != c)
    def _():
        from_z(0).wait_recv()

    total = zr[0].astype(F32)
    for i in range(1, 8):
        total = total + zr[i].astype(F32)
    gw[...] = total.astype(BF16)

    for group in ORDER:
        first, last = GROUPS[group]
        lanes = pl.ds(first * HS, (last - first) * HS)
        grads.wait(group)
        for which, out in ((0, dk), (1, dv)):
            out[:, lanes] = (
                down[which, :, lanes]
                + drecv[0, which, :, lanes].astype(F32)
                + drecv[1, which, :, lanes].astype(F32)
            ).astype(BF16)
    for copy in copies.started:
        copy.wait_send()
    keys_values.drain()
    grads.drain()
    for p in (0, 1):
        for half in range(2):
            for b in (0, 1):
                mine, at, copy = to_owner(p, half, b)

                @pl.when(jnp.logical_not(mine))
                def _():
                    copy.wait_send()


def on_device(queries, keys, values, grad_out, out_weight, frame_clip):
    vmem = pl.BlockSpec(memory_space=pltpu.VMEM)
    hbm = pl.BlockSpec(memory_space=pl.ANY)
    half = jax.ShapeDtypeStruct((ROWS, HD), BF16)
    edge = [pltpu.SemaphoreType.DMA((n,)) for n in (20, 20, 4, 4, 4)]
    res, dq, dk, dv, gw = pl.pallas_call(
        body,
        out_shape=(
            jax.ShapeDtypeStruct((ROWS, 8 * BLOCK), BF16),
            half,
            half,
            half,
            jax.ShapeDtypeStruct((64, 512), BF16),
        ),
        in_specs=[vmem, hbm, hbm, vmem, vmem, pl.BlockSpec(memory_space=pltpu.SMEM)],
        out_specs=(vmem,) * 5,
        scratch_shapes=[
            pltpu.VMEM((3 * ROWS, HD), BF16),
            pltpu.VMEM((3 * ROWS, HD), BF16),
            pltpu.VMEM((8 * BLOCK, HD), BF16),
            pltpu.VMEM((8, 3 * ROWS), F32),
            pltpu.VMEM((HEADS, ROWS, 3 * ROWS), BF16),
            pltpu.VMEM((2, ROWS, HD), BF16),
            pltpu.VMEM((ROWS, HD), BF16),
            pltpu.VMEM((ROWS, WIDE), BF16),
            pltpu.VMEM((2, 2, ROWS, HD), BF16),
            pltpu.VMEM((2, 2, ROWS, HD), BF16),
            pltpu.VMEM((2, ROWS, HD), F32),
            pltpu.VMEM((2, 2, ROWS, 2 * HS), BF16),
            pltpu.VMEM((2, 2, ROWS, 2 * HS), BF16),
            pltpu.VMEM((2, HD, HALF), BF16),
            pltpu.VMEM((2, 2, 208, HALF), BF16),
            pltpu.VMEM((2, 2, 416, HALF), BF16),
            pltpu.VMEM((432, HALF), F32),
            pltpu.VMEM((2, 4, 2, 64, HALF), BF16),
            pltpu.VMEM((2, 3, 2, 64, HALF), BF16),
            pltpu.VMEM((8, 64, 512), BF16),
            pltpu.VMEM((8, 64, 512), BF16),
            pltpu.SemaphoreType.DMA((2,)),
            pltpu.SemaphoreType.DMA((N_COPIES,)),
            pltpu.SemaphoreType.DMA((N_COPIES,)),
            pltpu.SemaphoreType.DMA((8,)),
            pltpu.SemaphoreType.DMA((8,)),
        ] + edge + edge,
        compiler_params=pltpu.CompilerParams(
            collective_id=0, has_side_effects=True, vmem_limit_bytes=63 * 1024 * 1024
        ),
        cost_estimate=pl.CostEstimate(flops=12_100_000_000, bytes_accessed=25_000_000, transcendentals=2_600_000),
        name="attention_and_projection",
    )(queries[0], keys[0], values[0], grad_out[0], out_weight, frame_clip)
    return (res[None], dq[None], dk[None], dv[None], gw[:52, :BLOCK])


def solution(mesh):
    in_specs = (
        P("dp", "tm", None),
        P("dp", "tm", None),
        P("dp", "tm", None),
        P("dp", "tm", None),
        P(None, "dp"),
        P("dp", None),
    )
    out_specs = (
        P("dp", "tm", None),
        P("dp", "tm", None),
        P("dp", "tm", None),
        P("dp", "tm", None),
        P("tm", "dp"),
    )
    return jax.shard_map(
        on_device, mesh=mesh, in_specs=in_specs, out_specs=out_specs, check_vma=False
    )
```

time: 290 us -> 244 us (0.84)
  Pallas kernels: 267 us -> 228 us
  local copies, waits for them, and re-layouts: 16.3 us -> 11 us
    pallas_call x1, Pallas kernels: 267 us -> 228 us  [on_device(): pl.pallas_call(body, out_shape=(jax.ShapeDtypeStruct((ROWS, 8 * BLOCK), B...]
    unnamed x15 -> x11, local copies, waits for them, and re-layouts: 8.7 us -> 9.54 us
where the time goes in v2:
time: 244 us; the launch traced here: 239 us
  Pallas kernels  228 us (93%)
  local copies, waits for them, and re-layouts  11 us (5%)
    pallas_call x1, Pallas kernels, on_device(): pl.pallas_call(body, out_shape=(jax.ShapeDtypeStruct((ROWS, 8 * BLOCK), B...  228 us
    unnamed x11, local copies, waits for them, and re-layouts  9.54 us

profile of v2, /device:TPU:37, one launch (start us, length us, event | category | flops | bytes accessed | tf_op | source)
XLA Modules:
  0.0 239.2 jit_solution(16342312775746893836)
XLA Ops:
  0.6 3.5 %copy.11.weight = bf16[1664,400]{1,0:T(8,128)(2,1)} copy(bf16[1664,400]{0,1:T(8,128)(2,1)} %param.10) | data formatting | bytes 2662400 | tf_op args[4]
  4.1 227.5 %attention_and_projection.1 = (bf16[256,3200]{1,0:T(8,128)(2,1)}, bf16[256,1664]{1,0:T(8,128)(2,1)}, bf16[256,1664]{1,0:T(8,128)(2,1)}, bf16[256,1664]{1,0:T(8,128)(2,1)}, bf16[64,512]{1,0:T(8,128)(2,1)}) custom-call(bf16[256,1664]{1,0:T(8,128)(2,1)} %bitcast.13, bf16[256,1664]{1,0:T(8,128)(2,1)} %bitcast.14, bf16[256,1664]{1,0:T(8,128)(2,1)} %bitcast.15, ...), custom_call_target="tpu_custom_call" | custom-call | flops 12099999744 | bytes 25000000 | tf_op jit(solution)/shard_map/attention_and_projection/pallas_call | solution.py:453
  231.7 1.4 slice.3
  233.1 0.0 copy-start.2
  233.1 2.8 %copy.16 = bf16[1,256,3200]{2,1,0:T(8,128)(2,1)} copy(bf16[1,256,3200]{2,1,0:T(8,128)(2,1)} %bitcast.8) | data formatting | bytes 3276800
  235.9 0.0 copy-done.2
  235.9 0.0 copy-start.1
  235.9 0.0 copy-start
  235.9 0.9 copy.17
  236.8 0.6 copy-done.1
  237.4 0.9 copy.18
  238.3 0.0 copy-done
  238.3 0.9 copy.19
Async XLA Ops:
  233.1 2.8 %copy-start.2 = (bf16[256,1664]{1,0:T(8,128)(2,1)S(1)}, bf16[256,1664]{1,0:T(8,128)(2,1)}, u32[]{:S(2)}) copy-start(bf16[256,1664]{1,0:T(8,128)(2,1)} %get-tuple-element.11) | copy-start | bytes 2555908
  235.9 1.5 copy-start.1
  235.9 2.4 copy-start

commit v3 on v2

--- a/solution.py
+++ b/solution.py
@@ -58,7 +58,7 @@
     return lax.dot_general(a, b, (((1,), (0,)), ((), ())), preferred_element_type=F32)
 
 
-N_COPIES = 47
+N_COPIES = 45
 
 
 class Beside:
@@ -187,6 +187,9 @@
     along_y = [place(x, lax.rem(y + d, 4), z, c) for d in (1, 2, 3)]
     along_z = [place(x, y, lax.rem(z + d, 8), c) for d in range(1, 8)]
     across_z = [place(x, y, lax.rem(z + d, 8), 1 - c) for d in range(1, 8)]
+    step_free, step_full = 3 - 2 * zh, 1 + 2 * zh
+    y_free, y_full = lax.rem(y + step_free, 4), lax.rem(y + step_full, 4)
+    free, full = place(x, y_free, z, c), place(x, y_full, z, c)
     partners = [up, down_dev, peer] + along_x + along_y + along_z + across_z
 
     barrier = pltpu.get_barrier_semaphore()
@@ -203,8 +206,8 @@
     own_k.start()
     own_v.start()
     own = pl.ds(pl.multiple_of(dp * BLOCK, 16), BLOCK)
-    for h in range(HEADS):
-        w[own, h * HS : (h + 1) * HS] = weight[h * HS : (h + 1) * HS, :].T
+    own_w = pltpu.make_async_copy(weight, w.at[own], local.at[2])
+    own_w.start()
     here = clip[0, tm]
     before_off = jnp.where(jnp.logical_and(tm > 0, clip[0, lax.rem(tm + 31, 32)] == here), 0.0, -1e30).astype(F32)
     after_off = jnp.where(jnp.logical_and(tm < 31, clip[0, lax.rem(tm + 1, 32)] == here), 0.0, -1e30).astype(F32)
@@ -243,21 +246,20 @@
     w_z = []
     second = place(x, y, lax.rem(z + 2 + 4 * c, 8), c)
     for device in (along_z[0], along_z[6], second):
-        w_z.append(same(piece_at(dp, y), device))
-        w_z.append(same(rest_at(dp), device))
+        mine = weight.at[pl.ds(pl.multiple_of(y * PIECE, 16), PIECE)]
+        w_z.append(copies.start(mine, piece_at(dp, y), device))
+        w_z.append(copies.start(weight.at[pl.ds(4 * PIECE, REST)], rest_at(dp), device))
     for group in (3, 4):
         keys_values.start_into(group)
     keys_values.start_inner(ORDER)
-    w_peer = [same(w.at[own], peer)]
+    w_peer = [copies.start(weight, w.at[own], peer)]
     go_peer = copies.start(go.at[:, pl.ds(pl.multiple_of(1536 * (1 - c), 128), WIDE)], gop, peer)
 
     others = [lax.rem(zl + d, 4) * 2 + c for d in (1, 2, 3)]
     for copy in w_z:
         copy.wait_recv()
-    w_y = []
-    for device in along_y:
-        for block in others:
-            w_y.append(same(piece_at(block, y), device))
+    w_free = [same(piece_at(block, y), free) for block in others]
+    w_full = [same(piece_at(block, y), full) for block in others]
     keys_values.start_over((0, 1, 2))
     for block in others:
         w_peer.append(same(piece_at(block, y), peer))
@@ -266,6 +268,7 @@
 
     own_k.wait()
     own_v.wait()
+    own_w.wait()
 
     def forward(h, carry):
         lanes = pl.ds(pl.multiple_of(h * HS, HS), HS)
@@ -276,15 +279,22 @@
         mx[0, :, lanes] = nn(p, vw[:, lanes]).astype(BF16)
         return carry
 
-    def w_along_y():
-        for i, d in enumerate((1, 2, 3)):
-            for j, block in enumerate(others):
-                w_y[3 * i + j].wait_recv()
-                w_peer.append(same(piece_at(block, lax.rem(y + 4 - d, 4)), peer))
+    def w_arrived(sent, from_y):
+        for block, copy in zip(others, sent):
+            copy.wait_recv()
+            w_peer.append(same(piece_at(block, from_y), peer))
 
     for index, group in enumerate(ORDER):
+        if index == 2:
+            w_free[0].wait_recv()
+            w_free[1].wait_recv()
+            w_free[2].wait_recv()
+            w_on = [same(piece_at(block, y_full), free) for block in others]
+            for block in others:
+                w_peer.append(same(piece_at(block, y_full), peer))
         if index == 4:
-            w_along_y()
+            w_arrived(w_full, y_free)
+            w_arrived(w_on, lax.rem(y + 2, 4))
         keys_values.wait(group)
         lax.fori_loop(*GROUPS[group], forward, 0)
     mx_peer = copies.start(mx.at[0], mx.at[1], peer)
@@ -292,12 +302,9 @@
     go_peer.wait_recv()
     mx_peer.wait_recv()
 
-    def chunk(p, at, half=None):
-        if half is None:
-            return term.at[p, pl.ds(pl.multiple_of(at * 416, 16), 416)]
-        return term.at[p, pl.ds(pl.multiple_of(at * 416 + half * 208, 16), 208)]
-
-    after, across, before = [lax.rem(y + d, 4) for d in (1, 2, 3)]
+    def chunk(p, at):
+        return term.at[p, pl.ds(pl.multiple_of(at * 416, 16), 416)]
+
     y_first, y_second, x_copies = [], [], []
     for p in (0, 1):
         def weight_term(h, carry):
@@ -309,19 +316,14 @@
             return carry
 
         lax.fori_loop(0, HEADS, weight_term, 0)
-        y_first.append([
-            copies.start(chunk(p, across, 0), yr1.at[p, 0], along_y[0]),
-            copies.start(chunk(p, across, 1), yr1.at[p, 1], along_y[2]),
-        ])
+        y_first.append(copies.start(chunk(p, lax.rem(y + 2, 4)), yr1.at[p], free))
+        y_second.append([copies.start(chunk(p, y_full), yr2.at[p, 1], full)])
 
     def y_next(p):
-        pair = []
-        for half, target, device in ((0, after, along_y[0]), (1, before, along_y[2])):
-            y_first[p][half].wait_recv()
-            part = chunk(p, target, half)
-            part[...] = (part[...].astype(F32) + yr1[p, half].astype(F32)).astype(BF16)
-            pair.append(copies.start(chunk(p, target), yr2.at[p, half], device))
-        y_second.append(pair)
+        y_first[p].wait_recv()
+        part = chunk(p, y_free)
+        part[...] = (part[...].astype(F32) + yr1[p].astype(F32)).astype(BF16)
+        y_second[p].append(copies.start(part, yr2.at[p, 0], free))
 
     for copy in w_peer:
         copy.wait_recv()
@@ -349,12 +351,13 @@
         else:
             grads.start_over((group,))
         grads.start_inner((group,))
-        if index in (1, 3):
-            y_next(index // 2)
+        if index == 4:
+            y_next(0)
 
     for i in range(5):
         columns = pl.ds(i * 640, 640)
         res[:, columns] = nt(mx[0], w[columns, :]).astype(BF16)
+    y_next(1)
     grads.pass_on()
 
     for p in (0, 1):
@@ -459,7 +462,7 @@
             half,
             jax.ShapeDtypeStruct((64, 512), BF16),
         ),
-        in_specs=[vmem, hbm, hbm, vmem, vmem, pl.BlockSpec(memory_space=pltpu.SMEM)],
+        in_specs=[vmem, hbm, hbm, vmem, hbm, pl.BlockSpec(memory_space=pltpu.SMEM)],
         out_specs=(vmem,) * 5,
         scratch_shapes=[
             pltpu.VMEM((3 * ROWS, HD), BF16),
@@ -476,14 +479,14 @@
             pltpu.VMEM((2, 2, ROWS, 2 * HS), BF16),
             pltpu.VMEM((2, 2, ROWS, 2 * HS), BF16),
             pltpu.VMEM((2, HD, HALF), BF16),
-            pltpu.VMEM((2, 2, 208, HALF), BF16),
+            pltpu.VMEM((2, 416, HALF), BF16),
             pltpu.VMEM((2, 2, 416, HALF), BF16),
             pltpu.VMEM((432, HALF), F32),
             pltpu.VMEM((2, 4, 2, 64, HALF), BF16),
             pltpu.VMEM((2, 3, 2, 64, HALF), BF16),
             pltpu.VMEM((8, 64, 512), BF16),
             pltpu.VMEM((8, 64, 512), BF16),
-            pltpu.SemaphoreType.DMA((2,)),
+            pltpu.SemaphoreType.DMA((3,)),
             pltpu.SemaphoreType.DMA((N_COPIES,)),
             pltpu.SemaphoreType.DMA((N_COPIES,)),
             pltpu.SemaphoreType.DMA((8,)),
@@ -494,7 +497,7 @@
         ),
         cost_estimate=pl.CostEstimate(flops=12_100_000_000, bytes_accessed=25_000_000, transcendentals=2_600_000),
         name="attention_and_projection",
-    )(queries[0], keys[0], values[0], grad_out[0], out_weight, frame_clip)
+    )(queries[0], keys[0], values[0], grad_out[0], out_weight.T, frame_clip)
     return (res[None], dq[None], dk[None], dv[None], gw[:52, :BLOCK])
 
 

time: 244 us -> 203 us (0.83)
  the two profiles are of different devices: /device:TPU:37 before, /device:TPU:1 now
where the time goes in v3:
time: 203 us
  Pallas kernels  195 us (96%)
  local copies, waits for them, and re-layouts  7.5 us (4%)
    pallas_call x1, Pallas kernels, on_device(): pl.pallas_call(body, out_shape=(jax.ShapeDtypeStruct((ROWS, 8 * BLOCK), B...  195 us
    unnamed x10, local copies, waits for them, and re-layouts  6.05 us

profile of v3, /device:TPU:1, one launch (start us, length us, event | category | flops | bytes accessed | tf_op | source)
XLA Modules:
  0.0 202.7 jit_solution(10196421346437157458)
XLA Ops:
  0.6 194.5 %attention_and_projection.1 = (bf16[256,3200]{1,0:T(8,128)(2,1)}, bf16[256,1664]{1,0:T(8,128)(2,1)}, bf16[256,1664]{1,0:T(8,128)(2,1)}, bf16[256,1664]{1,0:T(8,128)(2,1)}, bf16[64,512]{1,0:T(8,128)(2,1)}) custom-call(bf16[256,1664]{1,0:T(8,128)(2,1)} %bitcast.15, bf16[256,1664]{1,0:T(8,128)(2,1)} %bitcast.16, bf16[256,1664]{1,0:T(8,128)(2,1)} %bitcast.17, ...), custom_call_target="tpu_custom_call" | custom-call | flops 12099999744 | bytes 25000000 | tf_op jit(solution)/shard_map/attention_and_projection/pallas_call | solution.py:456
  195.2 1.4 slice.3
  196.6 0.0 copy-start.2
  196.6 2.8 %copy.15 = bf16[1,256,3200]{2,1,0:T(8,128)(2,1)} copy(bf16[1,256,3200]{2,1,0:T(8,128)(2,1)} %bitcast.9) | data formatting | bytes 3276800
  199.4 0.0 copy-done.2
  199.4 0.0 copy-start.1
  199.4 0.0 copy-start
  199.4 0.9 copy.16
  200.3 0.6 copy-done.1
  200.9 0.9 copy.17
  201.8 0.0 copy-done
  201.8 0.9 copy.18
Async XLA Ops:
  196.6 2.8 %copy-start.2 = (bf16[256,1664]{1,0:T(8,128)(2,1)S(1)}, bf16[256,1664]{1,0:T(8,128)(2,1)}, u32[]{:S(2)}) copy-start(bf16[256,1664]{1,0:T(8,128)(2,1)} %get-tuple-element.11) | copy-start | bytes 2555908
  199.4 1.5 copy-start.1
  199.4 2.4 %copy-start = (bf16[256,1664]{1,0:T(8,128)(2,1)S(1)}, bf16[256,1664]{1,0:T(8,128)(2,1)}, u32[]{:S(2)}) copy-start(bf16[256,1664]{1,0:T(8,128)(2,1)} %get-tuple-element.13) | copy-start | bytes 2555908

commit v4 on v3

--- a/solution.py
+++ b/solution.py
@@ -15,8 +15,11 @@
 BLOCK = 400
 PIECE = 96
 REST = 16
-GROUPS = ((0, 3), (3, 6), (6, 9), (9, 11), (11, 13))
+GROUPS = ((0, 3), (3, 5), (5, 7), (7, 10), (10, 13))
 ORDER = (3, 4, 0, 1, 2)
+ARRIVAL = (0, 1, 3, 4, 2)
+VIA = 3 * HS
+LONG = 320
 HALF = 896
 WIDE = 1664
 MESH = pl.DeviceIdType.MESH
@@ -58,7 +61,7 @@
     return lax.dot_general(a, b, (((1,), (0,)), ((), ())), preferred_element_type=F32)
 
 
-N_COPIES = 45
+N_COPIES = 52
 
 
 class Beside:
@@ -251,7 +254,7 @@
         w_z.append(copies.start(weight.at[pl.ds(4 * PIECE, REST)], rest_at(dp), device))
     for group in (3, 4):
         keys_values.start_into(group)
-    keys_values.start_inner(ORDER)
+    keys_values.start_inner(ARRIVAL[:2])
     w_peer = [copies.start(weight, w.at[own], peer)]
     go_peer = copies.start(go.at[:, pl.ds(pl.multiple_of(1536 * (1 - c), 128), WIDE)], gop, peer)
 
@@ -261,6 +264,7 @@
     w_free = [same(piece_at(block, y), free) for block in others]
     w_full = [same(piece_at(block, y), full) for block in others]
     keys_values.start_over((0, 1, 2))
+    keys_values.start_inner(ARRIVAL[2:])
     for block in others:
         w_peer.append(same(piece_at(block, y), peer))
         w_peer.append(same(rest_at(block), peer))
@@ -279,22 +283,26 @@
         mx[0, :, lanes] = nn(p, vw[:, lanes]).astype(BF16)
         return carry
 
-    def w_arrived(sent, from_y):
-        for block, copy in zip(others, sent):
+    def w_arrived(blocks, sent, from_y):
+        for block, copy in zip(blocks, sent):
             copy.wait_recv()
             w_peer.append(same(piece_at(block, from_y), peer))
 
-    for index, group in enumerate(ORDER):
-        if index == 2:
-            w_free[0].wait_recv()
-            w_free[1].wait_recv()
-            w_free[2].wait_recv()
-            w_on = [same(piece_at(block, y_full), free) for block in others]
+    for index, group in enumerate(ARRIVAL):
+        if index == 1:
+            w_on = []
+            for i, (block, copy) in enumerate(zip(others, w_free)):
+                copy.wait_recv()
+                if i < 2:
+                    w_on.append(same(piece_at(block, y_full), free))
+            w_full[2].wait_recv()
+            w_on.append(same(piece_at(others[2], y_free), full))
             for block in others:
                 w_peer.append(same(piece_at(block, y_full), peer))
+            w_peer.append(same(piece_at(others[2], y_free), peer))
         if index == 4:
-            w_arrived(w_full, y_free)
-            w_arrived(w_on, lax.rem(y + 2, 4))
+            w_arrived(others[:2], w_full[:2], y_free)
+            w_arrived(others, w_on, lax.rem(y + 2, 4))
         keys_values.wait(group)
         lax.fori_loop(*GROUPS[group], forward, 0)
     mx_peer = copies.start(mx.at[0], mx.at[1], peer)
@@ -305,6 +313,13 @@
     def chunk(p, at):
         return term.at[p, pl.ds(pl.multiple_of(at * 416, 16), 416)]
 
+    def near(p, at):
+        return term.at[p, pl.ds(pl.multiple_of(at * 416, 16), LONG)]
+
+    def far(p, at):
+        return term.at[p, pl.ds(pl.multiple_of(at * 416 + LONG, 16), 416 - LONG)]
+
+    opposite = lax.rem(y + 2, 4)
     y_first, y_second, x_copies = [], [], []
     for p in (0, 1):
         def weight_term(h, carry):
@@ -316,14 +331,23 @@
             return carry
 
         lax.fori_loop(0, HEADS, weight_term, 0)
-        y_first.append(copies.start(chunk(p, lax.rem(y + 2, 4)), yr1.at[p], free))
-        y_second.append([copies.start(chunk(p, y_full), yr2.at[p, 1], full)])
+        y_first.append((
+            copies.start(near(p, opposite), yr1.at[p, pl.ds(0, LONG)], free),
+            copies.start(far(p, opposite), yr1.at[p, pl.ds(LONG, 416 - LONG)], full),
+        ))
+        y_second.append([
+            copies.start(near(p, y_full), yr2.at[p, 1, pl.ds(0, LONG)], full),
+            copies.start(far(p, y_free), yr2.at[p, 0, pl.ds(LONG, 416 - LONG)], free),
+        ])
 
     def y_next(p):
-        y_first[p].wait_recv()
-        part = chunk(p, y_free)
-        part[...] = (part[...].astype(F32) + yr1[p].astype(F32)).astype(BF16)
-        y_second[p].append(copies.start(part, yr2.at[p, 0], free))
+        for copy, part, rows, side, device in (
+            (y_first[p][1], far(p, y_full), pl.ds(LONG, 416 - LONG), 1, full),
+            (y_first[p][0], near(p, y_free), pl.ds(0, LONG), 0, free),
+        ):
+            copy.wait_recv()
+            part[...] = (part[...].astype(F32) + yr1[p, rows].astype(F32)).astype(BF16)
+            y_second[p].append(copies.start(part, yr2.at[p, side, rows], device))
 
     for copy in w_peer:
         copy.wait_recv()
@@ -373,6 +397,17 @@
         x_copies.append([
             copies.start(xs.at[p, lax.rem(x + d, 4)], xr.at[p, d - 1], along_x[d - 1]) for d in (1, 2, 3)
         ])
+
+    def add_beside(group):
+        first, last = GROUPS[group]
+        lanes = pl.ds(first * HS, (last - first) * HS)
+        grads.wait(group)
+        for which, out in ((0, dk), (1, dv)):
+            out[:, lanes] = (
+                down[which, :, lanes]
+                + drecv[0, which, :, lanes].astype(F32)
+                + drecv[1, which, :, lanes].astype(F32)
+            ).astype(BF16)
 
     def to_owner(p, half, b):
         at = p * 4 + half * 2 + b
@@ -406,6 +441,9 @@
                 def _():
                     copy.start()
 
+        for group in ((3, 4), (0, 1, 2))[p]:
+            add_beside(group)
+
     def from_z(slot):
         return pltpu.make_async_remote_copy(
             src_ref=zs.at[0], dst_ref=zr.at[slot], send_sem=z_send.at[0], recv_sem=z_recv.at[slot],
@@ -422,18 +460,8 @@
     total = zr[0].astype(F32)
     for i in range(1, 8):
         total = total + zr[i].astype(F32)
-    gw[...] = total.astype(BF16)
-
-    for group in ORDER:
-        first, last = GROUPS[group]
-        lanes = pl.ds(first * HS, (last - first) * HS)
-        grads.wait(group)
-        for which, out in ((0, dk), (1, dv)):
-            out[:, lanes] = (
-                down[which, :, lanes]
-                + drecv[0, which, :, lanes].astype(F32)
-                + drecv[1, which, :, lanes].astype(F32)
-            ).astype(BF16)
+    gw[...] = total[:52, :BLOCK].astype(BF16)
+
     for copy in copies.started:
         copy.wait_send()
     keys_values.drain()
@@ -446,6 +474,33 @@
                 @pl.when(jnp.logical_not(mine))
                 def _():
                     copy.wait_send()
+
+
+PARTS = 4
+
+
+def put_out(*refs):
+    ins, outs, held = refs[:5], refs[5:10], refs[10:15]
+    in_sem, out_sem = refs[15:]
+    steps = []
+    for i, (src, dst, via) in enumerate(zip(ins, outs, held)):
+        parts = PARTS if i < 4 else 1
+        rows = src.shape[0] // parts
+        for j in range(parts):
+            at = pl.ds(j * rows, rows)
+            n = len(steps)
+            a, b, c = (src, via, dst) if parts == 1 else (src.at[at], via.at[at], dst.at[at])
+            steps.append((
+                pltpu.make_async_copy(a, b, in_sem.at[n]),
+                pltpu.make_async_copy(b, c, out_sem.at[n]),
+            ))
+    for first, _ in steps:
+        first.start()
+    for first, second in steps:
+        first.wait()
+        second.start()
+    for _, second in steps:
+        second.wait()
 
 
 def on_device(queries, keys, values, grad_out, out_weight, frame_clip):
@@ -460,7 +515,7 @@
             half,
             half,
             half,
-            jax.ShapeDtypeStruct((64, 512), BF16),
+            jax.ShapeDtypeStruct((52, BLOCK), BF16),
         ),
         in_specs=[vmem, hbm, hbm, vmem, hbm, pl.BlockSpec(memory_space=pltpu.SMEM)],
         out_specs=(vmem,) * 5,
@@ -476,8 +531,8 @@
             pltpu.VMEM((2, 2, ROWS, HD), BF16),
             pltpu.VMEM((2, 2, ROWS, HD), BF16),
             pltpu.VMEM((2, ROWS, HD), F32),
-            pltpu.VMEM((2, 2, ROWS, 2 * HS), BF16),
-            pltpu.VMEM((2, 2, ROWS, 2 * HS), BF16),
+            pltpu.VMEM((2, 2, ROWS, VIA), BF16),
+            pltpu.VMEM((2, 2, ROWS, VIA), BF16),
             pltpu.VMEM((2, HD, HALF), BF16),
             pltpu.VMEM((2, 416, HALF), BF16),
             pltpu.VMEM((2, 2, 416, HALF), BF16),
@@ -498,7 +553,18 @@
         cost_estimate=pl.CostEstimate(flops=12_100_000_000, bytes_accessed=25_000_000, transcendentals=2_600_000),
         name="attention_and_projection",
     )(queries[0], keys[0], values[0], grad_out[0], out_weight.T, frame_clip)
-    return (res[None], dq[None], dk[None], dv[None], gw[:52, :BLOCK])
+    outs = (res, dq, dk, dv, gw)
+    res, dq, dk, dv, gw = pl.pallas_call(
+        put_out,
+        out_shape=tuple(jax.ShapeDtypeStruct(a.shape, a.dtype) for a in outs),
+        in_specs=[hbm] * 5,
+        out_specs=(hbm,) * 5,
+        scratch_shapes=[pltpu.VMEM(a.shape, a.dtype) for a in outs]
+        + [pltpu.SemaphoreType.DMA((4 * PARTS + 1,)), pltpu.SemaphoreType.DMA((4 * PARTS + 1,))],
+        compiler_params=pltpu.CompilerParams(vmem_limit_bytes=60 * 1024 * 1024),
+        name="outputs",
+    )(*outs)
+    return (res[None], dq[None], dk[None], dv[None], gw)
 
 
 def solution(mesh):

time: 203 us -> 214 us (1.054)
  the two profiles are of different devices: /device:TPU:1 before, /device:TPU:37 now
where the time goes in v4:
time: 214 us
  Pallas kernels  213 us (100%)
    pallas_call x1, Pallas kernels, on_device(): pl.pallas_call(body, out_shape=(jax.ShapeDtypeStruct((ROWS, 8 * BLOCK), B...  210 us

profile of v4, /device:TPU:37, one launch (start us, length us, event | category | flops | bytes accessed | tf_op | source)
XLA Modules:
  0.0 214.3 jit_solution(8665748021578455953)
XLA Ops:
  0.6 209.8 %attention_and_projection.1 = (bf16[256,3200]{1,0:T(8,128)(2,1)}, bf16[256,1664]{1,0:T(8,128)(2,1)}, bf16[256,1664]{1,0:T(8,128)(2,1)}, bf16[256,1664]{1,0:T(8,128)(2,1)}, bf16[52,400]{1,0:T(8,128)(2,1)}) custom-call(bf16[256,1664]{1,0:T(8,128)(2,1)} %bitcast.12, bf16[256,1664]{1,0:T(8,128)(2,1)} %bitcast.13, bf16[256,1664]{1,0:T(8,128)(2,1)} %bitcast.14, ...), custom_call_target="tpu_custom_call" | custom-call | flops 12099999744 | bytes 25000000 | tf_op jit(solution)/shard_map/attention_and_projection/pallas_call | solution.py:511
  210.4 3.7 %outputs.1 = (bf16[256,3200]{1,0:T(8,128)(2,1)}, bf16[256,1664]{1,0:T(8,128)(2,1)}, bf16[256,1664]{1,0:T(8,128)(2,1)}, bf16[256,1664]{1,0:T(8,128)(2,1)}, bf16[52,400]{1,0:T(8,128)(2,1)}) custom-call(bf16[256,3200]{1,0:T(8,128)(2,1)} %get-tuple-element.15.refs_0_, bf16[256,1664]{1,0:T(8,128)(2,1)} %get-tuple-element.16.refs_1_, ...), custom_call_target="tpu_custom_call" | custom-call | tf_op jit(solution)/shard_map/outputs/pallas_call | solution.py:557

commit v5 on v3

--- a/solution.py
+++ b/solution.py
@@ -15,7 +15,7 @@
 BLOCK = 400
 PIECE = 96
 REST = 16
-GROUPS = ((0, 3), (3, 6), (6, 9), (9, 11), (11, 13))
+GROUPS = ((6, 9), (3, 6), (0, 3), (9, 11), (11, 13))
 ORDER = (3, 4, 0, 1, 2)
 HALF = 896
 WIDE = 1664
@@ -58,7 +58,7 @@
     return lax.dot_general(a, b, (((1,), (0,)), ((), ())), preferred_element_type=F32)
 
 
-N_COPIES = 45
+N_COPIES = 42
 
 
 class Beside:
@@ -164,9 +164,9 @@
 def body(
     q, k, v, go, weight, clip,
     res, dq, dk, dv, gw,
-    kw, vw, w, bias, probs, mx, gm, gop, dsend, drecv, down, held_kv, held_grad,
-    term, yr1, yr2, ysum, xs, xr, zs, zr,
-    local, send, recv, z_send, z_recv, *edge_sems,
+    kw, vw, w, bias, probs, mx, mxs, gm, gos, dsend, drecv, down, held_kv, held_grad,
+    term, yr, ysum, xs, xr, zs, zr,
+    local, send, recv, z_send, z_recv, mx_send, mx_recv, *edge_sems,
 ):
     tm = lax.axis_index("tm")
     dp = lax.axis_index("dp")
@@ -184,17 +184,26 @@
     down_dev = (lax.rem(tm + 31, 32), dp)
     peer = place(x, y, z, 1 - c)
     along_x = [place(lax.rem(x + d, 4), y, z, c) for d in (1, 2, 3)]
-    along_y = [place(x, lax.rem(y + d, 4), z, c) for d in (1, 2, 3)]
-    along_z = [place(x, y, lax.rem(z + d, 8), c) for d in range(1, 8)]
-    across_z = [place(x, y, lax.rem(z + d, 8), 1 - c) for d in range(1, 8)]
+    along_z = [place(x, y, lax.rem(z + d, 8), c) for d in (1, 2, 6, 7)]
+    half_of = lax.rem((y + 1) // 2, 2)
+    beside_y = y + 1 - 2 * (y % 2)
+    beside, beside_peer = place(x, beside_y, z, c), place(x, beside_y, z, 1 - c)
+    same_half = place(x, 3 - y, z, c)
+    from_y = jnp.where(y % 2 == 0, 2 * (zl // 2), 3 - 2 * (zl // 2))
+    from_c = y // 2
+    own_part = jnp.logical_and(from_c == c, from_y == y)
     step_free, step_full = 3 - 2 * zh, 1 + 2 * zh
     y_free, y_full = lax.rem(y + step_free, 4), lax.rem(y + step_full, 4)
     free, full = place(x, y_free, z, c), place(x, y_full, z, c)
-    partners = [up, down_dev, peer] + along_x + along_y + along_z + across_z
+    partners = [up, down_dev, peer, free, full, beside_peer] + along_x + along_z
 
     barrier = pltpu.get_barrier_semaphore()
     for device in partners:
         pl.semaphore_signal(barrier, inc=1, device_id=device, device_id_type=MESH)
+    for z_from in range(8):
+        @pl.when(jnp.logical_not(jnp.logical_and(own_part, z_from == z)))
+        def _():
+            pl.semaphore_signal(barrier, inc=1, device_id=place(x, from_y, z_from, from_c), device_id_type=MESH)
     for column, step in ((0, -1), (3, 1)):
         @pl.when(x == column)
         def _():
@@ -232,7 +241,8 @@
         lambda which, lanes: (dsend.at[0, which, :, lanes], drecv.at[0, which, :, lanes]),
         held_grad, edge_sems[5:],
     )
-    pl.semaphore_wait(barrier, len(partners) + 2 * jnp.logical_or(x == 1, x == 2).astype(jnp.int32))
+    signals = len(partners) + 8 - own_part.astype(jnp.int32) + 2 * jnp.logical_or(x == 1, x == 2).astype(jnp.int32)
+    pl.semaphore_wait(barrier, signals)
 
     def piece_at(block, at):
         return w.at[pl.ds(pl.multiple_of(block * BLOCK + at * PIECE, 16), PIECE)]
@@ -243,9 +253,13 @@
     def same(ref, device):
         return copies.start(ref, ref, device)
 
+    def go_half(which):
+        return go.at[:, pl.ds(pl.multiple_of(1536 * which, 128), WIDE)]
+
+    go_beside = copies.start(go_half(1 - half_of), gos.at[1], beside)
     w_z = []
     second = place(x, y, lax.rem(z + 2 + 4 * c, 8), c)
-    for device in (along_z[0], along_z[6], second):
+    for device in (along_z[0], along_z[3], second):
         mine = weight.at[pl.ds(pl.multiple_of(y * PIECE, 16), PIECE)]
         w_z.append(copies.start(mine, piece_at(dp, y), device))
         w_z.append(copies.start(weight.at[pl.ds(4 * PIECE, REST)], rest_at(dp), device))
@@ -253,7 +267,7 @@
         keys_values.start_into(group)
     keys_values.start_inner(ORDER)
     w_peer = [copies.start(weight, w.at[own], peer)]
-    go_peer = copies.start(go.at[:, pl.ds(pl.multiple_of(1536 * (1 - c), 128), WIDE)], gop, peer)
+    go_peer = [copies.start(go_half(half_of), gos.at[0], peer)]
 
     others = [lax.rem(zl + d, 4) * 2 + c for d in (1, 2, 3)]
     for copy in w_z:
@@ -264,6 +278,8 @@
     for block in others:
         w_peer.append(same(piece_at(block, y), peer))
         w_peer.append(same(rest_at(block), peer))
+    go_beside.wait_recv()
+    go_peer.append(copies.start(gos.at[1], gos.at[2], peer))
     keys_values.pass_on()
 
     own_k.wait()
@@ -276,8 +292,38 @@
         e = jnp.exp2(s - jnp.max(s, axis=-1, keepdims=True))
         p = (e * (1.0 / jnp.sum(e, axis=-1, keepdims=True))).astype(BF16)
         probs[h] = p
-        mx[0, :, lanes] = nn(p, vw[:, lanes]).astype(BF16)
+        mx[:, lanes] = nn(p, vw[:, lanes]).astype(BF16)
         return carry
+
+    def mixed_to(window, part):
+        first, size = ((384, 512), (0, 384))[part]
+        src = mx.at[:, 768 * window + first : 768 * window + first + size]
+        slot = jnp.where(c == window, 1, 2)
+        here = pl.ds(first, size)
+        at = (window * 2 + part) * 2
+        return (
+            pltpu.make_async_remote_copy(
+                src_ref=src, dst_ref=mxs.at[slot, :, here], send_sem=mx_send.at[at], recv_sem=mx_recv.at[slot * 2 + part],
+                device_id=place(x, beside_y, z, window), device_id_type=MESH),
+            pltpu.make_async_remote_copy(
+                src_ref=src, dst_ref=mxs.at[0, :, here], send_sem=mx_send.at[at + 1], recv_sem=mx_recv.at[part],
+                device_id=peer, device_id_type=MESH),
+        )
+
+    def send_mixed(window, part):
+        outside, inside = mixed_to(window, part)
+        outside.start()
+
+        @pl.when(c != window)
+        def _():
+            inside.start()
+
+    def wait_mixed(slot, part):
+        first, size = ((384, 512), (0, 384))[part]
+        here = pl.ds(first, size)
+        pltpu.make_async_remote_copy(
+            src_ref=mx.at[:, here], dst_ref=mxs.at[slot, :, here], send_sem=mx_send.at[0], recv_sem=mx_recv.at[slot * 2 + part],
+            device_id=peer, device_id_type=MESH).wait_recv()
 
     def w_arrived(sent, from_y):
         for block, copy in zip(others, sent):
@@ -297,33 +343,43 @@
             w_arrived(w_on, lax.rem(y + 2, 4))
         keys_values.wait(group)
         lax.fori_loop(*GROUPS[group], forward, 0)
-    mx_peer = copies.start(mx.at[0], mx.at[1], peer)
-
-    go_peer.wait_recv()
-    mx_peer.wait_recv()
-
-    def chunk(p, at):
-        return term.at[p, pl.ds(pl.multiple_of(at * 416, 16), 416)]
-
-    y_first, y_second, x_copies = [], [], []
+        if index > 0:
+            send_mixed(*((1, 0), (1, 1), (0, 0), (0, 1))[index - 1])
+
+    for copy in go_peer:
+        copy.wait_recv()
+    for part in (0, 1):
+        for slot in range(3):
+            wait_mixed(slot, part)
+
+    def chunk(p, parity):
+        return term.at[p, pl.ds(pl.multiple_of(64 * c + 416 * parity, 16), 416)]
+
+    y_copies, x_copies = [], []
     for p in (0, 1):
         def weight_term(h, carry):
+            own_lanes = pl.ds(pl.multiple_of((6 * c + h) * HS, HS), HS)
             lanes = pl.ds(pl.multiple_of(h * HS, HS), HS)
-            columns = pl.ds(pl.multiple_of(1536 * c + 768 * p, 128), HALF)
-            term[p, lanes, :] = (
-                tn(mx[0, :, lanes], go[:, columns]) + tn(mx[1, :, lanes], gop[:, 768 * p : 768 * p + HALF])
-            ).astype(BF16)
+            columns = pl.ds(pl.multiple_of(1536 * half_of + 768 * p, 128), HALF)
+            total = tn(mx[:, own_lanes], go[:, columns])
+            for i in range(3):
+                total = total + tn(mxs[i, :, lanes], gos[i, :, 768 * p : 768 * p + HALF])
+            term[p, lanes, :] = total.astype(BF16)
             return carry
 
-        lax.fori_loop(0, HEADS, weight_term, 0)
-        y_first.append(copies.start(chunk(p, lax.rem(y + 2, 4)), yr1.at[p], free))
-        y_second.append([copies.start(chunk(p, y_full), yr2.at[p, 1], full)])
-
-    def y_next(p):
-        y_first[p].wait_recv()
-        part = chunk(p, y_free)
-        part[...] = (part[...].astype(F32) + yr1[p].astype(F32)).astype(BF16)
-        y_second[p].append(copies.start(part, yr2.at[p, 0], free))
+        lax.fori_loop(0, 7, weight_term, 0)
+        y_copies.append(copies.start(chunk(p, 1 - y % 2), yr.at[p], same_half))
+
+    def sum_y(p):
+        y_copies[p].wait_recv()
+        ysum[pl.ds(0, 416), :] = chunk(p, y % 2)[...].astype(F32) + yr[p].astype(F32)
+        ysum[pl.ds(416, 16), :] = jnp.zeros((16, HALF), F32)
+        for to in range(4):
+            for half in range(2):
+                xs[p, to, half] = ysum[pl.ds(208 * half + 52 * to, 64), :].astype(BF16)
+        x_copies.append([
+            copies.start(xs.at[p, lax.rem(x + d, 4)], xr.at[p, d - 1], along_x[d - 1]) for d in (1, 2, 3)
+        ])
 
     for copy in w_peer:
         copy.wait_recv()
@@ -332,7 +388,7 @@
         lanes = pl.ds(pl.multiple_of(h * HS, HS), HS)
         g = gm[:, lanes]
         p = probs[h]
-        delta = jnp.sum(g.astype(F32) * mx[0, :, lanes].astype(F32), axis=-1, keepdims=True)
+        delta = jnp.sum(g.astype(F32) * mx[:, lanes].astype(F32), axis=-1, keepdims=True)
         ds = (p.astype(F32) * (nt(g, vw[:, lanes]) - delta)).astype(BF16)
         dq[:, lanes] = (nn(ds, kw[:, lanes]) * SCALE).astype(BF16)
         for which, grad in ((0, tn(ds, q[:, lanes]) * SCALE), (1, tn(p, g))):
@@ -352,36 +408,23 @@
             grads.start_over((group,))
         grads.start_inner((group,))
         if index == 4:
-            y_next(0)
+            sum_y(0)
 
     for i in range(5):
         columns = pl.ds(i * 640, 640)
-        res[:, columns] = nt(mx[0], w[columns, :]).astype(BF16)
-    y_next(1)
+        res[:, columns] = nt(mx[...], w[columns, :]).astype(BF16)
+    sum_y(1)
     grads.pass_on()
-
-    for p in (0, 1):
-        for copy in y_second[p]:
-            copy.wait_recv()
-        ysum[pl.ds(0, 416), :] = (
-            chunk(p, y)[...].astype(F32) + yr2[p, 0].astype(F32) + yr2[p, 1].astype(F32)
-        )
-        ysum[pl.ds(416, 16), :] = jnp.zeros((16, HALF), F32)
-        for to in range(4):
-            for half in range(2):
-                xs[p, to, half] = ysum[pl.ds(208 * half + 52 * to, 64), :].astype(BF16)
-        x_copies.append([
-            copies.start(xs.at[p, lax.rem(x + d, 4)], xr.at[p, d - 1], along_x[d - 1]) for d in (1, 2, 3)
-        ])
 
     def to_owner(p, half, b):
         at = p * 4 + half * 2 + b
-        z_to = half * 4 + c * 2 + p
+        z_to = half * 4 + half_of * 2 + p
         slot = lax.rem(z + 8 - z_to, 8)
-        mine = jnp.logical_and(z_to == z, c == b)
+        y_to = 2 * c + y % 2
+        mine = jnp.logical_and(jnp.logical_and(z_to == z, y_to == y), c == b)
         return mine, at, pltpu.make_async_remote_copy(
             src_ref=zs.at[at], dst_ref=zr.at[slot], send_sem=z_send.at[at], recv_sem=z_recv.at[slot],
-            device_id=place(x, y, z_to, b), device_id_type=MESH,
+            device_id=place(x, y_to, z_to, b), device_id_type=MESH,
         )
 
     for p in (0, 1):
@@ -392,7 +435,7 @@
             for i in range(3):
                 total = total + xr[p, i, half].astype(F32)
             for b in (0, 1):
-                shift = lax.rem(2 * HALF - BLOCK * b - 32 * p - 64 * c, HALF)
+                shift = lax.rem(2 * HALF - BLOCK * b - 32 * p - 64 * half_of, HALF)
                 zs[p * 4 + half * 2 + b] = pltpu.roll(total, shift, 1)[:, :512].astype(BF16)
         for half in range(2):
             for b in (0, 1):
@@ -411,18 +454,6 @@
             src_ref=zs.at[0], dst_ref=zr.at[slot], send_sem=z_send.at[0], recv_sem=z_recv.at[slot],
             device_id=peer, device_id_type=MESH,
         )
-
-    for slot in range(1, 8):
-        from_z(slot).wait_recv()
-
-    @pl.when(zl // 2 != c)
-    def _():
-        from_z(0).wait_recv()
-
-    total = zr[0].astype(F32)
-    for i in range(1, 8):
-        total = total + zr[i].astype(F32)
-    gw[...] = total.astype(BF16)
 
     for group in ORDER:
         first, last = GROUPS[group]
@@ -434,8 +465,29 @@
                 + drecv[0, which, :, lanes].astype(F32)
                 + drecv[1, which, :, lanes].astype(F32)
             ).astype(BF16)
+    for slot in range(1, 8):
+        from_z(slot).wait_recv()
+
+    @pl.when(jnp.logical_not(own_part))
+    def _():
+        from_z(0).wait_recv()
+
+    total = zr[0].astype(F32)
+    for i in range(1, 8):
+        total = total + zr[i].astype(F32)
+    gw[...] = total[:52, :BLOCK].astype(BF16)
+
     for copy in copies.started:
         copy.wait_send()
+    for window in (0, 1):
+        for part in (0, 1):
+            outside, inside = mixed_to(window, part)
+            outside.wait_send()
+
+            @pl.when(c != window)
+            def _():
+                inside.wait_send()
+
     keys_values.drain()
     grads.drain()
     for p in (0, 1):
@@ -446,6 +498,33 @@
                 @pl.when(jnp.logical_not(mine))
                 def _():
                     copy.wait_send()
+
+
+PARTS = 4
+
+
+def put_out(*refs):
+    ins, outs, held = refs[:5], refs[5:10], refs[10:15]
+    in_sem, out_sem = refs[15:]
+    steps = []
+    for i, (src, dst, via) in enumerate(zip(ins, outs, held)):
+        parts = PARTS if i < 4 else 1
+        rows = src.shape[0] // parts
+        for j in range(parts):
+            at = pl.ds(j * rows, rows)
+            n = len(steps)
+            a, b, c = (src, via, dst) if parts == 1 else (src.at[at], via.at[at], dst.at[at])
+            steps.append((
+                pltpu.make_async_copy(a, b, in_sem.at[n]),
+                pltpu.make_async_copy(b, c, out_sem.at[n]),
+            ))
+    for first, _ in steps:
+        first.start()
+    for first, second in steps:
+        first.wait()
+        second.start()
+    for _, second in steps:
+        second.wait()
 
 
 def on_device(queries, keys, values, grad_out, out_weight, frame_clip):
@@ -460,7 +539,7 @@
             half,
             half,
             half,
-            jax.ShapeDtypeStruct((64, 512), BF16),
+            jax.ShapeDtypeStruct((52, BLOCK), BF16),
         ),
         in_specs=[vmem, hbm, hbm, vmem, hbm, pl.BlockSpec(memory_space=pltpu.SMEM)],
         out_specs=(vmem,) * 5,
@@ -470,17 +549,17 @@
             pltpu.VMEM((8 * BLOCK, HD), BF16),
             pltpu.VMEM((8, 3 * ROWS), F32),
             pltpu.VMEM((HEADS, ROWS, 3 * ROWS), BF16),
-            pltpu.VMEM((2, ROWS, HD), BF16),
             pltpu.VMEM((ROWS, HD), BF16),
-            pltpu.VMEM((ROWS, WIDE), BF16),
+            pltpu.VMEM((3, ROWS, HALF), BF16),
+            pltpu.VMEM((ROWS, HD), BF16),
+            pltpu.VMEM((3, ROWS, WIDE), BF16),
             pltpu.VMEM((2, 2, ROWS, HD), BF16),
             pltpu.VMEM((2, 2, ROWS, HD), BF16),
             pltpu.VMEM((2, ROWS, HD), F32),
             pltpu.VMEM((2, 2, ROWS, 2 * HS), BF16),
             pltpu.VMEM((2, 2, ROWS, 2 * HS), BF16),
-            pltpu.VMEM((2, HD, HALF), BF16),
+            pltpu.VMEM((2, HALF, HALF), BF16),
             pltpu.VMEM((2, 416, HALF), BF16),
-            pltpu.VMEM((2, 2, 416, HALF), BF16),
             pltpu.VMEM((432, HALF), F32),
             pltpu.VMEM((2, 4, 2, 64, HALF), BF16),
             pltpu.VMEM((2, 3, 2, 64, HALF), BF16),
@@ -491,6 +570,8 @@
             pltpu.SemaphoreType.DMA((N_COPIES,)),
             pltpu.SemaphoreType.DMA((8,)),
             pltpu.SemaphoreType.DMA((8,)),
+            pltpu.SemaphoreType.DMA((8,)),
+            pltpu.SemaphoreType.DMA((6,)),
         ] + edge + edge,
         compiler_params=pltpu.CompilerParams(
             collective_id=0, has_side_effects=True, vmem_limit_bytes=63 * 1024 * 1024
@@ -498,7 +579,18 @@
         cost_estimate=pl.CostEstimate(flops=12_100_000_000, bytes_accessed=25_000_000, transcendentals=2_600_000),
         name="attention_and_projection",
     )(queries[0], keys[0], values[0], grad_out[0], out_weight.T, frame_clip)
-    return (res[None], dq[None], dk[None], dv[None], gw[:52, :BLOCK])
+    outs = (res, dq, dk, dv, gw)
+    res, dq, dk, dv, gw = pl.pallas_call(
+        put_out,
+        out_shape=tuple(jax.ShapeDtypeStruct(a.shape, a.dtype) for a in outs),
+        in_specs=[hbm] * 5,
+        out_specs=(hbm,) * 5,
+        scratch_shapes=[pltpu.VMEM(a.shape, a.dtype) for a in outs]
+        + [pltpu.SemaphoreType.DMA((4 * PARTS + 1,)), pltpu.SemaphoreType.DMA((4 * PARTS + 1,))],
+        compiler_params=pltpu.CompilerParams(vmem_limit_bytes=60 * 1024 * 1024),
+        name="outputs",
+    )(*outs)
+    return (res[None], dq[None], dk[None], dv[None], gw)
 
 
 def solution(mesh):

time: 203 us -> 207 us (1.020)
  the two profiles are of different devices: /device:TPU:1 before, /device:TPU:45 now
where the time goes in v5:
time: 207 us
  Pallas kernels  206 us (100%)
    pallas_call x1, Pallas kernels, on_device(): pl.pallas_call(body, out_shape=(jax.ShapeDtypeStruct((ROWS, 8 * BLOCK), B...  202 us

profile of v5, /device:TPU:45, one launch (start us, length us, event | category | flops | bytes accessed | tf_op | source)
XLA Modules:
  0.0 206.6 jit_solution(17712841642553463499)
XLA Ops:
  0.6 202.1 %attention_and_projection.1 = (bf16[256,3200]{1,0:T(8,128)(2,1)}, bf16[256,1664]{1,0:T(8,128)(2,1)}, bf16[256,1664]{1,0:T(8,128)(2,1)}, bf16[256,1664]{1,0:T(8,128)(2,1)}, bf16[52,400]{1,0:T(8,128)(2,1)}) custom-call(bf16[256,1664]{1,0:T(8,128)(2,1)} %bitcast.12, bf16[256,1664]{1,0:T(8,128)(2,1)} %bitcast.13, bf16[256,1664]{1,0:T(8,128)(2,1)} %bitcast.14, ...), custom_call_target="tpu_custom_call" | custom-call | flops 12099999744 | bytes 25000000 | tf_op jit(solution)/shard_map/attention_and_projection/pallas_call | solution.py:535
  202.7 3.7 %outputs.1 = (bf16[256,3200]{1,0:T(8,128)(2,1)}, bf16[256,1664]{1,0:T(8,128)(2,1)}, bf16[256,1664]{1,0:T(8,128)(2,1)}, bf16[256,1664]{1,0:T(8,128)(2,1)}, bf16[52,400]{1,0:T(8,128)(2,1)}) custom-call(bf16[256,3200]{1,0:T(8,128)(2,1)} %get-tuple-element.15.refs_0_, bf16[256,1664]{1,0:T(8,128)(2,1)} %get-tuple-element.16.refs_1_, ...), custom_call_target="tpu_custom_call" | custom-call | tf_op jit(solution)/shard_map/outputs/pallas_call | solution.py:583

commit v6 on v3

--- a/solution.py
+++ b/solution.py
@@ -18,6 +18,7 @@
 GROUPS = ((0, 3), (3, 6), (6, 9), (9, 11), (11, 13))
 ORDER = (3, 4, 0, 1, 2)
 HALF = 896
+WIDTH = (896, 768)
 WIDE = 1664
 MESH = pl.DeviceIdType.MESH
 F32 = jnp.float32
@@ -165,7 +166,7 @@
     q, k, v, go, weight, clip,
     res, dq, dk, dv, gw,
     kw, vw, w, bias, probs, mx, gm, gop, dsend, drecv, down, held_kv, held_grad,
-    term, yr1, yr2, ysum, xs, xr, zs, zr,
+    term, yr1, yr2, ysum, edge, xs, xr, zs, zr,
     local, send, recv, z_send, z_recv, *edge_sems,
 ):
     tm = lax.axis_index("tm")
@@ -251,6 +252,7 @@
         w_z.append(copies.start(weight.at[pl.ds(4 * PIECE, REST)], rest_at(dp), device))
     for group in (3, 4):
         keys_values.start_into(group)
+    keys_values.start_over((0, 1, 2))
     keys_values.start_inner(ORDER)
     w_peer = [copies.start(weight, w.at[own], peer)]
     go_peer = copies.start(go.at[:, pl.ds(pl.multiple_of(1536 * (1 - c), 128), WIDE)], gop, peer)
@@ -260,7 +262,6 @@
         copy.wait_recv()
     w_free = [same(piece_at(block, y), free) for block in others]
     w_full = [same(piece_at(block, y), full) for block in others]
-    keys_values.start_over((0, 1, 2))
     for block in others:
         w_peer.append(same(piece_at(block, y), peer))
         w_peer.append(same(rest_at(block), peer))
@@ -284,17 +285,13 @@
             copy.wait_recv()
             w_peer.append(same(piece_at(block, from_y), peer))
 
+    w_free[0].wait_recv()
+    w_free[1].wait_recv()
+    w_free[2].wait_recv()
+    w_on = [same(piece_at(block, y_full), free) for block in others]
+    for block in others:
+        w_peer.append(same(piece_at(block, y_full), peer))
     for index, group in enumerate(ORDER):
-        if index == 2:
-            w_free[0].wait_recv()
-            w_free[1].wait_recv()
-            w_free[2].wait_recv()
-            w_on = [same(piece_at(block, y_full), free) for block in others]
-            for block in others:
-                w_peer.append(same(piece_at(block, y_full), peer))
-        if index == 4:
-            w_arrived(w_full, y_free)
-            w_arrived(w_on, lax.rem(y + 2, 4))
         keys_values.wait(group)
         lax.fori_loop(*GROUPS[group], forward, 0)
     mx_peer = copies.start(mx.at[0], mx.at[1], peer)
@@ -303,28 +300,36 @@
     mx_peer.wait_recv()
 
     def chunk(p, at):
-        return term.at[p, pl.ds(pl.multiple_of(at * 416, 16), 416)]
-
+        return term.at[p, pl.ds(pl.multiple_of(at * 416, 16), 416), pl.ds(0, WIDTH[p])]
+
+    opposite = lax.rem(y + 2, 4)
     y_first, y_second, x_copies = [], [], []
     for p in (0, 1):
-        def weight_term(h, carry):
+        first, size = HALF * p, WIDTH[p]
+
+        def weight_term(step, carry):
+            h = lax.rem((opposite * HEADS) // 4 + step, HEADS)
             lanes = pl.ds(pl.multiple_of(h * HS, HS), HS)
-            columns = pl.ds(pl.multiple_of(1536 * c + 768 * p, 128), HALF)
-            term[p, lanes, :] = (
-                tn(mx[0, :, lanes], go[:, columns]) + tn(mx[1, :, lanes], gop[:, 768 * p : 768 * p + HALF])
+            columns = pl.ds(pl.multiple_of(1536 * c + first, 128), size)
+            term[p, lanes, 0:size] = (
+                tn(mx[0, :, lanes], go[:, columns]) + tn(mx[1, :, lanes], gop[:, first : first + size])
             ).astype(BF16)
             return carry
 
-        lax.fori_loop(0, HEADS, weight_term, 0)
-        y_first.append(copies.start(chunk(p, lax.rem(y + 2, 4)), yr1.at[p], free))
-        y_second.append([copies.start(chunk(p, y_full), yr2.at[p, 1], full)])
+        lax.fori_loop(0, 4, weight_term, 0)
+        y_first.append(copies.start(chunk(p, opposite), yr1.at[p, :, pl.ds(0, size)], free))
+        lax.fori_loop(4, HEADS, weight_term, 0)
+        y_second.append([copies.start(chunk(p, y_full), yr2.at[p, 1, :, pl.ds(0, size)], full)])
 
     def y_next(p):
         y_first[p].wait_recv()
         part = chunk(p, y_free)
-        part[...] = (part[...].astype(F32) + yr1[p].astype(F32)).astype(BF16)
-        y_second[p].append(copies.start(part, yr2.at[p, 0], free))
-
+        here = pl.ds(0, WIDTH[p])
+        part[...] = (part[...].astype(F32) + yr1[p, :, here].astype(F32)).astype(BF16)
+        y_second[p].append(copies.start(part, yr2.at[p, 0, :, here], free))
+
+    w_arrived(w_full, y_free)
+    w_arrived(w_on, lax.rem(y + 2, 4))
     for copy in w_peer:
         copy.wait_recv()
 
@@ -357,21 +362,23 @@
     for i in range(5):
         columns = pl.ds(i * 640, 640)
         res[:, columns] = nt(mx[0], w[columns, :]).astype(BF16)
+    grads.pass_on()
     y_next(1)
-    grads.pass_on()
 
     for p in (0, 1):
         for copy in y_second[p]:
             copy.wait_recv()
-        ysum[pl.ds(0, 416), :] = (
-            chunk(p, y)[...].astype(F32) + yr2[p, 0].astype(F32) + yr2[p, 1].astype(F32)
+        here = pl.ds(0, WIDTH[p])
+        ysum[pl.ds(0, 416), here] = (
+            chunk(p, y)[...].astype(F32) + yr2[p, 0, :, here].astype(F32) + yr2[p, 1, :, here].astype(F32)
         )
         ysum[pl.ds(416, 16), :] = jnp.zeros((16, HALF), F32)
         for to in range(4):
             for half in range(2):
-                xs[p, to, half] = ysum[pl.ds(208 * half + 52 * to, 64), :].astype(BF16)
+                xs[p, to, half, :, here] = ysum[pl.ds(208 * half + 52 * to, 64), here].astype(BF16)
         x_copies.append([
-            copies.start(xs.at[p, lax.rem(x + d, 4)], xr.at[p, d - 1], along_x[d - 1]) for d in (1, 2, 3)
+            copies.start(xs.at[p, lax.rem(x + d, 4), :, :, here], xr.at[p, d - 1, :, :, here], along_x[d - 1])
+            for d in (1, 2, 3)
         ])
 
     def to_owner(p, half, b):
@@ -388,9 +395,14 @@
         for copy in x_copies[p]:
             copy.wait_recv()
         for half in range(2):
-            total = xs[p, x, half].astype(F32)
+            here = pl.ds(0, WIDTH[p])
+            total = xs[p, x, half, :, here].astype(F32)
             for i in range(3):
-                total = total + xr[p, i, half].astype(F32)
+                total = total + xr[p, i, half, :, here].astype(F32)
+            if p == 0:
+                edge[half] = total[:, 768:]
+            else:
+                total = jnp.concatenate([edge[half], total], axis=1)
             for b in (0, 1):
                 shift = lax.rem(2 * HALF - BLOCK * b - 32 * p - 64 * c, HALF)
                 zs[p * 4 + half * 2 + b] = pltpu.roll(total, shift, 1)[:, :512].astype(BF16)
@@ -422,7 +434,7 @@
     total = zr[0].astype(F32)
     for i in range(1, 8):
         total = total + zr[i].astype(F32)
-    gw[...] = total.astype(BF16)
+    gw[...] = total[:52, :BLOCK].astype(BF16)
 
     for group in ORDER:
         first, last = GROUPS[group]
@@ -448,6 +460,33 @@
                     copy.wait_send()
 
 
+PARTS = 4
+
+
+def put_out(*refs):
+    ins, outs, held = refs[:5], refs[5:10], refs[10:15]
+    in_sem, out_sem = refs[15:]
+    steps = []
+    for i, (src, dst, via) in enumerate(zip(ins, outs, held)):
+        parts = PARTS if i < 4 else 1
+        rows = src.shape[0] // parts
+        for j in range(parts):
+            at = pl.ds(j * rows, rows)
+            n = len(steps)
+            a, b, c = (src, via, dst) if parts == 1 else (src.at[at], via.at[at], dst.at[at])
+            steps.append((
+                pltpu.make_async_copy(a, b, in_sem.at[n]),
+                pltpu.make_async_copy(b, c, out_sem.at[n]),
+            ))
+    for first, _ in steps:
+        first.start()
+    for first, second in steps:
+        first.wait()
+        second.start()
+    for _, second in steps:
+        second.wait()
+
+
 def on_device(queries, keys, values, grad_out, out_weight, frame_clip):
     vmem = pl.BlockSpec(memory_space=pltpu.VMEM)
     hbm = pl.BlockSpec(memory_space=pl.ANY)
@@ -460,7 +499,7 @@
             half,
             half,
             half,
-            jax.ShapeDtypeStruct((64, 512), BF16),
+            jax.ShapeDtypeStruct((52, BLOCK), BF16),
         ),
         in_specs=[vmem, hbm, hbm, vmem, hbm, pl.BlockSpec(memory_space=pltpu.SMEM)],
         out_specs=(vmem,) * 5,
@@ -482,6 +521,7 @@
             pltpu.VMEM((2, 416, HALF), BF16),
             pltpu.VMEM((2, 2, 416, HALF), BF16),
             pltpu.VMEM((432, HALF), F32),
+            pltpu.VMEM((2, 64, HS), F32),
             pltpu.VMEM((2, 4, 2, 64, HALF), BF16),
             pltpu.VMEM((2, 3, 2, 64, HALF), BF16),
             pltpu.VMEM((8, 64, 512), BF16),
@@ -498,7 +538,18 @@
         cost_estimate=pl.CostEstimate(flops=12_100_000_000, bytes_accessed=25_000_000, transcendentals=2_600_000),
         name="attention_and_projection",
     )(queries[0], keys[0], values[0], grad_out[0], out_weight.T, frame_clip)
-    return (res[None], dq[None], dk[None], dv[None], gw[:52, :BLOCK])
+    outs = (res, dq, dk, dv, gw)
+    res, dq, dk, dv, gw = pl.pallas_call(
+        put_out,
+        out_shape=tuple(jax.ShapeDtypeStruct(a.shape, a.dtype) for a in outs),
+        in_specs=[hbm] * 5,
+        out_specs=(hbm,) * 5,
+        scratch_shapes=[pltpu.VMEM(a.shape, a.dtype) for a in outs]
+        + [pltpu.SemaphoreType.DMA((4 * PARTS + 1,)), pltpu.SemaphoreType.DMA((4 * PARTS + 1,))],
+        compiler_params=pltpu.CompilerParams(vmem_limit_bytes=60 * 1024 * 1024),
+        name="outputs",
+    )(*outs)
+    return (res[None], dq[None], dk[None], dv[None], gw)
 
 
 def solution(mesh):

time: 203 us -> 195 us (0.961)
  the two profiles are of different devices: /device:TPU:1 before, /device:TPU:47 now
where the time goes in v6:
time: 195 us
  Pallas kernels  195 us (100%)
    pallas_call x1, Pallas kernels, on_device(): pl.pallas_call(body, out_shape=(jax.ShapeDtypeStruct((ROWS, 8 * BLOCK), B...  191 us

profile of v6, /device:TPU:47, one launch (start us, length us, event | category | flops | bytes accessed | tf_op | source)
XLA Modules:
  0.0 195.4 jit_solution(936196796874454969)
XLA Ops:
  0.6 190.8 %attention_and_projection.1 = (bf16[256,3200]{1,0:T(8,128)(2,1)}, bf16[256,1664]{1,0:T(8,128)(2,1)}, bf16[256,1664]{1,0:T(8,128)(2,1)}, bf16[256,1664]{1,0:T(8,128)(2,1)}, bf16[52,400]{1,0:T(8,128)(2,1)}) custom-call(bf16[256,1664]{1,0:T(8,128)(2,1)} %bitcast.12, bf16[256,1664]{1,0:T(8,128)(2,1)} %bitcast.13, bf16[256,1664]{1,0:T(8,128)(2,1)} %bitcast.14, ...), custom_call_target="tpu_custom_call" | custom-call | flops 12099999744 | bytes 25000000 | tf_op jit(solution)/shard_map/attention_and_projection/pallas_call | solution.py:495
  191.5 3.7 %outputs.1 = (bf16[256,3200]{1,0:T(8,128)(2,1)}, bf16[256,1664]{1,0:T(8,128)(2,1)}, bf16[256,1664]{1,0:T(8,128)(2,1)}, bf16[256,1664]{1,0:T(8,128)(2,1)}, bf16[52,400]{1,0:T(8,128)(2,1)}) custom-call(bf16[256,3200]{1,0:T(8,128)(2,1)} %get-tuple-element.15.refs_0_, bf16[256,1664]{1,0:T(8,128)(2,1)} %get-tuple-element.16.refs_1_, ...), custom_call_target="tpu_custom_call" | custom-call | tf_op jit(solution)/shard_map/outputs/pallas_call | solution.py:542
